TPU v7x, 32 devices: a whole 2x2x4 slice. The times are simulated.
32 devices in a mesh: fsdp: 4 (over x, core), ctx: 2 (over y), tp: 4 (over z).
Axes of the slice: x: 2, y: 2, z: 4, core: 2. Of those that a mesh axis runs over, the one named last changes fastest.
Arguments:
- latents: bfloat16 [4, 2048, 1152], P('fsdp', 'ctx'), may hold values from -6 to 6
- conditioning: bfloat16 [4, 1152], P('fsdp', 'tp'), may hold values from -6 to 6
- modulation_weight: bfloat16 [1152, 6, 1152], P('tp', None, ('fsdp', 'ctx')), may hold values from -0.1875 to 0.1875
- attention_weight: bfloat16 [1152, 3, 1152], P(('fsdp', 'ctx'), None, 'tp'), may hold values from -0.1875 to 0.1875
- output_weight: bfloat16 [1152, 1152], P('tp', ('fsdp', 'ctx')), may hold values from -3 to 3
- expand_weight: bfloat16 [1152, 4608], P(('fsdp', 'ctx'), 'tp'), may hold values from -0.1875 to 0.1875
- contract_weight: bfloat16 [4608, 1152], P('tp', ('fsdp', 'ctx')), may hold values from -0.09375 to 0.09375
- cotangent: bfloat16 [4, 2048, 1152], P('fsdp', 'ctx'), may hold values from -6 to 6
Outputs:
- block_out: bfloat16 [4, 2048, 1152], P('fsdp', 'ctx')
- latents_grad: bfloat16 [4, 2048, 1152], P('fsdp', 'ctx')
- conditioning_grad: float32 [4, 1152], P('fsdp', 'tp')
- modulation_grad: float32 [1152, 6, 1152], P('tp', None, ('fsdp', 'ctx'))
- attention_grad: float32 [1152, 3, 1152], P(('fsdp', 'ctx'), None, 'tp')
- output_grad: float32 [1152, 1152], P('tp', ('fsdp', 'ctx'))
- expand_grad: float32 [1152, 4608], P(('fsdp', 'ctx'), 'tp')
- contract_grad: float32 [4608, 1152], P('tp', ('fsdp', 'ctx'))
All inputs are finite; a program needn't handle non-finite values.
Results may differ from a plain program's by a relative error of at most 0.014.
The roundings to bfloat16 on the way count: a program that leaves them out, or rounds other values in their place, can miss the bound.
Values may be sent and summed in bfloat16 or wider, within the bound.
A program may use at most 192 MiB of HBM per device.

v0:
```python
from functools import partial

import jax
import jax.numpy as jnp
from jax import lax
from jax.sharding import PartitionSpec as P

HEAD_SIZE = 72


highest = lax.Precision.HIGHEST
epsilon = 1e-06


def layer_norm(value_rows):
    centred = value_rows - jnp.mean(value_rows, axis=-1, keepdims=True)
    spread = jnp.mean(centred * centred, axis=-1, keepdims=True)
    return centred * lax.rsqrt(spread + epsilon)


def modulate(value_rows, shift, scale):
    return layer_norm(value_rows) * (1.0 + scale[:, None, :]) + shift[:, None, :]


def head_major(value_rows):
    latent_count, row_count, width = value_rows.shape
    return value_rows.reshape(latent_count, row_count, width // HEAD_SIZE, HEAD_SIZE).transpose(
        2, 0, 1, 3
    )


def token_major(value_rows):
    head_count, latent_count, row_count, size = value_rows.shape
    return value_rows.transpose(1, 2, 0, 3).reshape(latent_count, row_count, head_count * size)


def forward_head(operands):
    query_matrix, key_rows, value_rows = operands
    logit_scores = jnp.einsum(
        "jxf,jrf->jxr", query_matrix, key_rows, preferred_element_type=jnp.float32
    ) * HEAD_SIZE ** (-0.5)
    top = jnp.max(logit_scores, axis=-1, keepdims=True)
    expo = jnp.exp(logit_scores - top)
    total = jnp.sum(expo, axis=-1, keepdims=True)
    probabilities = (expo / total).astype(jnp.bfloat16)
    mixed_values = jnp.einsum(
        "cms,csh->cmh", probabilities, value_rows, preferred_element_type=jnp.float32
    )
    return (mixed_values, (top + jnp.log(total))[..., 0])


def backward_head(operands):
    query_matrix, key_rows, value_rows, grad_mixed_rows, logsum = operands
    logit_scores = jnp.einsum(
        "jxf,jrf->jxr", query_matrix, key_rows, preferred_element_type=jnp.float32
    ) * HEAD_SIZE ** (-0.5)
    probabilities = jnp.exp(logit_scores - logsum[..., None])
    grad_probabilities = jnp.einsum(
        "jxf,jrf->jxr", grad_mixed_rows, value_rows, preferred_element_type=jnp.float32
    )
    inner = jnp.sum(probabilities * grad_probabilities, axis=-1, keepdims=True)
    grad_logit_scores = (probabilities * (grad_probabilities - inner)).astype(jnp.bfloat16)
    grad_query = jnp.einsum(
        "cms,csh->cmh", grad_logit_scores, key_rows, preferred_element_type=jnp.float32
    ) * HEAD_SIZE ** (-0.5)
    grad_keys = jnp.einsum(
        "vft,vfm->vtm", grad_logit_scores, query_matrix, preferred_element_type=jnp.float32
    ) * HEAD_SIZE ** (-0.5)
    grad_values = jnp.einsum(
        "vft,vfm->vtm",
        probabilities.astype(jnp.bfloat16),
        grad_mixed_rows,
        preferred_element_type=jnp.float32,
    )
    return (grad_query, grad_keys, grad_values)


def shards(
    latents,
    conditioning,
    modulation_weight,
    attention_weight,
    output_weight,
    expand_weight,
    contract_weight,
    cotangent,
):
    ada_full, qkv_full, out_full, expand_full, contract_full = (
        lax.all_gather(modulation_weight, ("fsdp", "ctx"), axis=2, tiled=True),
        lax.all_gather(attention_weight, ("fsdp", "ctx"), axis=0, tiled=True),
        lax.all_gather(output_weight, ("fsdp", "ctx"), axis=1, tiled=True),
        lax.all_gather(expand_weight, ("fsdp", "ctx"), axis=0, tiled=True),
        lax.all_gather(contract_weight, ("fsdp", "ctx"), axis=1, tiled=True),
    )
    share_rows = latents.shape[1] // lax.axis_size("tp")
    share_start = lax.axis_index("tp") * share_rows
    cond_float = conditioning.astype(jnp.float32)
    cond_silu, silu_pull = jax.vjp(jax.nn.silu, cond_float)
    cond_act = cond_silu.astype(jnp.bfloat16)
    modulations = lax.psum(
        jnp.einsum("bd,dkc->bkc", cond_act, ada_full, preferred_element_type=jnp.float32), "tp"
    )
    shift_one = modulations[:, 0]
    scale_one = modulations[:, 1]
    gate_one = modulations[:, 2]
    shift_two = modulations[:, 3]
    scale_two = modulations[:, 4]
    gate_two = modulations[:, 5]
    tokens_float = latents.astype(jnp.float32)
    token_share = lax.dynamic_slice_in_dim(tokens_float, share_start, share_rows, 1)
    act_one = modulate(tokens_float, shift_one, scale_one).astype(jnp.bfloat16)
    projected = jnp.einsum(
        "btd,dkc->btkc", act_one, qkv_full, preferred_element_type=jnp.float32
    ).astype(jnp.bfloat16)
    pair_local = projected[:, :, 1:]
    pair_all = lax.all_gather(pair_local, "ctx", axis=1, tiled=True)
    heads_query = head_major(projected[:, :, 0])
    keys_heads = head_major(pair_all[:, :, 0])
    values_heads = head_major(pair_all[:, :, 1])
    mixed_values, logsum = lax.map(forward_head, (heads_query, keys_heads, values_heads))
    attended = token_major(mixed_values).astype(jnp.bfloat16)
    branch_one = lax.psum_scatter(
        jnp.einsum("btc,cd->btd", attended, out_full, preferred_element_type=jnp.float32),
        "tp",
        scatter_dimension=1,
        tiled=True,
    )
    hidden = token_share + gate_one[:, None, :] * branch_one
    normed_two, norm_pull_two = jax.vjp(modulate, hidden, shift_two, scale_two)
    act_two = lax.all_gather(normed_two.astype(jnp.bfloat16), "tp", axis=1, tiled=True)
    pre_gelu = jnp.einsum("btd,df->btf", act_two, expand_full, preferred_element_type=jnp.float32)
    gelu_value, gelu_pull = jax.vjp(partial(jax.nn.gelu, approximate=True), pre_gelu)
    activated = gelu_value.astype(jnp.bfloat16)
    branch_two = lax.psum_scatter(
        jnp.einsum(
            "btf,fd->btd", activated, contract_full, preferred_element_type=jnp.float32
        ).astype(jnp.bfloat16),
        "tp",
        scatter_dimension=1,
        tiled=True,
    ).astype(jnp.float32)
    block_share = (hidden + gate_two[:, None, :] * branch_two).astype(jnp.bfloat16)
    ada_back, qkv_back, out_back, expand_back, contract_back = (
        lax.all_gather(modulation_weight, ("fsdp", "ctx"), axis=2, tiled=True),
        lax.all_gather(attention_weight, ("fsdp", "ctx"), axis=0, tiled=True),
        lax.all_gather(output_weight, ("fsdp", "ctx"), axis=1, tiled=True),
        lax.all_gather(expand_weight, ("fsdp", "ctx"), axis=0, tiled=True),
        lax.all_gather(contract_weight, ("fsdp", "ctx"), axis=1, tiled=True),
    )
    grad_out_full = cotangent.astype(jnp.float32)
    grad_out = lax.dynamic_slice_in_dim(grad_out_full, share_start, share_rows, 1)
    grad_gate_two = jnp.sum(grad_out * branch_two, axis=1)
    grad_branch_two = (grad_out_full * gate_two[:, None, :]).astype(jnp.bfloat16)
    grad_activated = jnp.einsum(
        "btd,fd->btf", grad_branch_two, contract_back, preferred_element_type=jnp.float32
    )
    grad_pre = gelu_pull(grad_activated)[0].astype(jnp.bfloat16)
    grad_contract = jnp.einsum(
        "btf,btd->fd", activated, grad_branch_two, preferred_element_type=jnp.float32
    )
    grad_act_two = lax.psum_scatter(
        jnp.einsum("btf,df->btd", grad_pre, expand_back, preferred_element_type=jnp.float32),
        "tp",
        scatter_dimension=1,
        tiled=True,
    )
    grad_expand = jnp.einsum("btd,btf->df", act_two, grad_pre, preferred_element_type=jnp.float32)
    grad_hidden, grad_shift_two, grad_scale_two = norm_pull_two(grad_act_two)
    grad_hidden = grad_hidden + grad_out
    grad_gate_one = jnp.sum(grad_hidden * branch_one, axis=1)
    branch_grad_share = (grad_hidden * gate_one[:, None, :]).astype(jnp.bfloat16)
    grad_branch_one = lax.all_gather(branch_grad_share, "tp", axis=1, tiled=True)
    grad_attended = jnp.einsum(
        "btd,cd->btc", grad_branch_one, out_back, preferred_element_type=jnp.float32
    ).astype(jnp.bfloat16)
    grad_output = jnp.einsum(
        "btc,btd->cd", attended, grad_branch_one, preferred_element_type=jnp.float32
    )
    heads_grad = head_major(grad_attended)
    grads_query, grads_keys, grads_values = lax.map(
        backward_head, (heads_query, keys_heads, values_heads, heads_grad, logsum)
    )
    pair_terms = jnp.stack((token_major(grads_keys), token_major(grads_values)), axis=2)
    grad_pair = lax.psum_scatter(pair_terms, "ctx", scatter_dimension=1, tiled=True).astype(
        jnp.bfloat16
    )
    grad_query = token_major(grads_query).astype(jnp.bfloat16)
    grad_projected = jnp.concatenate((grad_query[:, :, None], grad_pair), axis=2)
    grad_act_one = lax.psum_scatter(
        jnp.einsum("btkc,dkc->btd", grad_projected, qkv_back, preferred_element_type=jnp.float32),
        "tp",
        scatter_dimension=1,
        tiled=True,
    )
    grad_attention = jnp.einsum(
        "btd,btkc->dkc", act_one, grad_projected, preferred_element_type=jnp.float32
    )
    normed_share, norm_pull_one = jax.vjp(modulate, token_share, shift_one, scale_one)
    grad_tokens, grad_shift_one, grad_scale_one = norm_pull_one(grad_act_one)
    grad_tokens = grad_tokens + grad_hidden
    block_out, latents_grad = (
        lax.all_gather(block_share, "tp", axis=1, tiled=True),
        lax.all_gather(grad_tokens.astype(jnp.bfloat16), "tp", axis=1, tiled=True),
    )
    grad_parts = jnp.stack(
        (
            grad_shift_one,
            grad_scale_one,
            grad_gate_one,
            grad_shift_two,
            grad_scale_two,
            grad_gate_two,
        ),
        axis=1,
    )
    grad_modulations = lax.psum(grad_parts, ("ctx", "tp"))
    grad_modulation = jnp.einsum(
        "bd,bkc->dkc", cond_act.astype(jnp.float32), grad_modulations, precision=highest
    )
    grad_modulation = jnp.where(
        lax.axis_index("ctx") == 0, grad_modulation, jnp.zeros_like(grad_modulation)
    )
    grad_cond_act = jnp.einsum(
        "bkc,dkc->bd", grad_modulations, ada_back.astype(jnp.float32), precision=highest
    )
    conditioning_grad = silu_pull(grad_cond_act)[0]
    summed = (
        lax.psum_scatter(grad_modulation, ("fsdp", "ctx"), scatter_dimension=2, tiled=True),
        lax.psum_scatter(grad_attention, ("fsdp", "ctx"), scatter_dimension=0, tiled=True),
        lax.psum_scatter(grad_output, ("fsdp", "ctx"), scatter_dimension=1, tiled=True),
        lax.psum_scatter(grad_expand, ("fsdp", "ctx"), scatter_dimension=0, tiled=True),
        lax.psum_scatter(grad_contract, ("fsdp", "ctx"), scatter_dimension=1, tiled=True),
    )
    return (
        block_out,
        latents_grad,
        conditioning_grad,
        summed[0],
        summed[1],
        summed[2],
        summed[3],
        summed[4],
    )


def solution(mesh):
    return jax.shard_map(
        shards,
        mesh=mesh,
        in_specs=(
            P("fsdp", "ctx", None),
            P("fsdp", "tp"),
            P("tp", None, ("fsdp", "ctx")),
            P(("fsdp", "ctx"), None, "tp"),
            P("tp", ("fsdp", "ctx")),
            P(("fsdp", "ctx"), "tp"),
            P("tp", ("fsdp", "ctx")),
            P("fsdp", "ctx", None),
        ),
        out_specs=(
            P("fsdp", "ctx", None),
            P("fsdp", "ctx", None),
            P("fsdp", "tp"),
            P("tp", None, ("fsdp", "ctx")),
            P(("fsdp", "ctx"), None, "tp"),
            P("tp", ("fsdp", "ctx")),
            P(("fsdp", "ctx"), "tp"),
            P("tp", ("fsdp", "ctx")),
        ),
        check_vma=False,
    )
```

profile of v0, /device:TPU:0, one launch (start us, length us, event | category | flops | bytes accessed | tf_op | source)
XLA Modules:
  0.0 1233.1 jit_solution(2758197992182118360)
XLA Ops:
  11.6 42.4 %all-gather.10.cloned.1.call-done = bf16[288,6,1152]{0,2,1:T(8,128)(2,1)} async-done(((bf16[288,6,144]{0,2,1:T(8,128)(2,1)}), bf16[288,6,1152]{0,2,1:T(8,128)(2,1)}) %all-gather.10.cloned.1.call-update) | async-done | bytes 3981328 | tf_op jit(solution)/shard_map/all_gather | solution.py:89
  54.0 4.0 fusion.85
  58.0 19.4 %psum.14 = f32[1,6,1152]{2,1,0:T(8,128)S(1)} all-reduce(f32[1,6,1152]{2,1,0:T(8,128)S(1)} %copy.21), channel_id=1, replica_groups=mesh['fsdp'=4,'ctx'=2,'tp'=4] {'tp'}, use_global_device_ids=true, to_apply=%region_0.1 | all-reduce | flops 6912 | bytes 55296 | tf_op jit(solution)/shard_map/psum | solution.py:100
  77.5 8.7 all-gather.12.cloned.1.call-done
  86.2 4.5 convert_bitcast_fusion
  93.2 25.4 %all_gather.38 = bf16[288,1152]{0,1:T(8,128)(2,1)} all-gather(bf16[288,144]{0,1:T(8,128)(2,1)S(1)} %copy-done.21), channel_id=1, replica_groups=mesh['fsdp'=4,'ctx'=2,'tp'=4] {'fsdp','ctx'}, dimensions={1}, use_global_device_ids=true | all-gather | bytes 746496 | tf_op jit(solution)/shard_map/all_gather | solution.py:91
  119.3 14.7 %all-gather.14.cloned.1.call-done = bf16[1,2048,2,288]{1,3,2,0:T(8,128)(2,1)} async-done(((bf16[1,1024,2,288]{1,3,2,0:T(8,128)(2,1)}), bf16[1,2048,2,288]{1,3,2,0:T(8,128)(2,1)}) %all-gather.14.cloned.1.call-update) | async-done | bytes 2359312 | tf_op jit(solution)/shard_map/all_gather | solution.py:116
  133.9 3.3 fusion.99
  140.1 3.6 copy.18
  144.5 31.0 %while.26 = (s32[]{:T(128)}, bf16[4,1,1024,72]{2,3,1,0:T(8,128)(2,1)}, f32[4,1,1024]{2,1,0:T(1,128)S(1)}, bf16[4,1,1024,72]{3,2,1,0:T(8,128)(2,1)S(1)}, bf16[4,1...) while((s32[]{:T(128)}, bf16[4,1,1024,72]{2,3,1,0:T(8,128)(2,1)}, ...), condition=%wide.region_6.7_spmd, body=%wide.region_3.6_spmd.sunk | while | flops 622853120 | bytes 31533200 | solution.py:120
  147.8 3.6 fusion.133
  155.6 3.6 fusion.133
  163.3 3.6 fusion.133
  171.1 3.6 fusion.133
  175.5 5.4 convolution_bitcast_fusion.2
  181.6 4.1 convert_element_type.107
  187.2 79.2 %reduce-scatter.11.cloned.1.call-done = f32[1,256,1152]{2,1,0:T(8,128)} async-done(((f32[1,1024,1152]{2,1,0:T(8,128)}), f32[1,256,1152]{2,1,0:T(8,128)}) %reduce-scatter.11.cloned.1.call-update) | async-done | bytes 1179664 | tf_op jit(solution)/shard_map/reduce_scatter | solution.py:122
  271.3 27.6 %all-gather.18.cloned.1.call-done = bf16[1152,1152]{1,0:T(8,128)(2,1)} async-done(((bf16[144,1152]{1,0:T(8,128)(2,1)}), bf16[1152,1152]{1,0:T(8,128)(2,1)}) %all-gather.18.cloned.1.call-update) | async-done | bytes 2654224 | tf_op jit(solution)/shard_map/all_gather | solution.py:92
  298.9 52.5 %all-gather.16.cloned.1.call-done = bf16[1,1024,1152]{2,1,0:T(8,128)(2,1)} async-done(((bf16[1,256,1152]{2,1,0:T(8,128)(2,1)}), bf16[1,1024,1152]{2,1,0:T(8,128)(2,1)}) %all-gather.16.cloned.1.call-update) | async-done | bytes 2359312 | tf_op jit(solution)/shard_map/all_gather | solution.py:130
  351.4 8.1 fusion.65
  359.6 22.9 %all-gather.20.cloned.1.call-done = bf16[1152,1152]{0,1:T(8,128)(2,1)} async-done(((bf16[1152,144]{0,1:T(8,128)(2,1)}), bf16[1152,1152]{0,1:T(8,128)(2,1)}) %all-gather.20.cloned.1.call-update) | async-done | bytes 2654224 | tf_op jit(solution)/shard_map/all_gather | solution.py:93
  382.4 9.1 fusion.55
  392.9 5.2 convolution_bitcast_fusion.1
  398.2 8.8 fusion.56
  407.0 4.1 convert_element_type.122
  411.1 72.4 %reduce-scatter.15.cloned.1.call-done = f32[1,256,1152]{2,1,0:T(8,128)} async-done(((f32[1,1024,1152]{2,1,0:T(8,128)}), f32[1,256,1152]{2,1,0:T(8,128)}) %reduce-scatter.15.cloned.1.call-update) | async-done | bytes 1179664 | tf_op jit(solution)/shard_map/reduce_scatter | solution.py:161
  485.8 49.2 %reduce-scatter.13.cloned.1.call-done = bf16[1,256,1152]{2,1,0:T(8,128)(2,1)} async-done(((bf16[1,1024,1152]{2,1,0:T(8,128)(2,1)}), bf16[1,256,1152]{2,1,0:T(8,128)(2,1)}) %reduce-scatter.13.cloned.1.call-update) | async-done | bytes 589840 | tf_op jit(solution)/shard_map/reduce_scatter | solution.py:134
  542.5 49.6 %all-gather.24.cloned.1.call-done = bf16[1,1024,1152]{2,1,0:T(8,128)(2,1)} async-done(((bf16[1,256,1152]{2,1,0:T(8,128)(2,1)}), bf16[1,1024,1152]{2,1,0:T(8,128)(2,1)}) %all-gather.24.cloned.1.call-update) | async-done | bytes 2359312 | tf_op jit(solution)/shard_map/all_gather | solution.py:172
  592.1 3.7 fusion.67
  598.9 49.2 %while.27 = (s32[]{:T(128)}, bf16[4,1,1024,72]{2,3,1,0:T(8,128)(2,1)}, f32[4,1,2048,72]{2,3,1,0:T(8,128)}, f32[4,1,2048,72]{2,3,1,0:T(8,128)}, bf16[4,1,1024,72]...) while((s32[]{:T(128)}, ...), condition=%wide.region_16.17_spmd, body=%wide.region_14.16_spmd.sunk | while | flops 1535335424 | bytes 74122440 | solution.py:180
  639.5 3.2 multiply_reduce_fusion.13
  648.1 5.1 pad_maximum_fusion
  653.3 58.9 %reduce-scatter.17.cloned.1.call-done = f32[1,1024,2,288]{1,3,2,0:T(8,128)} async-done(((f32[1,2048,2,288]{1,3,2,0:T(8,128)}), f32[1,1024,2,288]{1,3,2,0:T(8,128)}) %reduce-scatter.17.cloned.1.call-update) | async-done | bytes 2359312 | tf_op jit(solution)/shard_map/reduce_scatter | solution.py:184
  715.1 5.3 convolution_bitcast_fusion
  721.2 84.6 %reduce-scatter.19.cloned.1.call-done = f32[1,256,1152]{2,1,0:T(8,128)} async-done(((f32[1,1024,1152]{2,1,0:T(8,128)}), f32[1,256,1152]{2,1,0:T(8,128)}) %reduce-scatter.19.cloned.1.call-update) | async-done | bytes 1179664 | tf_op jit(solution)/shard_map/reduce_scatter | solution.py:189
  812.1 8.1 fusion.73
  821.9 7.3 fusion.63
  829.3 4.7 fusion.59
  834.1 7.2 fusion.79
  842.2 38.8 %psum.15 = f32[6,1152]{1,0:T(8,128)S(1)} all-reduce(f32[6,1152]{1,0:T(8,128)S(1)} %bitcast.194), channel_id=1, replica_groups=mesh['fsdp'=4,'ctx'=2,'tp'=4] {'ctx','tp'}, use_global_device_ids=true, to_apply=%region_29.30 | all-reduce | flops 6912 | bytes 55296 | tf_op jit(solution)/shard_map/psum | solution.py:216
  881.0 4.5 multiply_select_fusion
  885.5 5.5 fusion.84
  890.9 19.6 %all-gather.26.cloned.1.call-done = bf16[1,1024,1152]{2,1,0:T(8,128)(2,1)} async-done(((bf16[1,256,1152]{2,1,0:T(8,128)(2,1)}), bf16[1,1024,1152]{2,1,0:T(8,128)(2,1)}) %all-gather.26.cloned.1.call-update) | async-done | bytes 2359312 | tf_op jit(solution)/shard_map/all_gather | solution.py:203
  910.5 60.0 %reduce-scatter.29.cloned.1.call-done = f32[1152,144]{0,1:T(8,128)} async-done(((f32[1152,1152]{0,1:T(8,128)}), f32[1152,144]{0,1:T(8,128)}) %reduce-scatter.29.cloned.1.call-update) | async-done | bytes 663568 | tf_op jit(solution)/shard_map/reduce_scatter | solution.py:232
  970.5 60.8 %reduce-scatter.27.cloned.1.call-done = f32[144,1152]{1,0:T(8,128)} async-done(((f32[1152,1152]{1,0:T(8,128)}), f32[144,1152]{1,0:T(8,128)}) %reduce-scatter.27.cloned.1.call-update) | async-done | bytes 663568 | tf_op jit(solution)/shard_map/reduce_scatter | solution.py:231
  1031.3 43.6 %reduce-scatter.25.cloned.1.call-done = f32[288,144]{0,1:T(8,128)} async-done(((f32[288,1152]{0,1:T(8,128)}), f32[288,144]{0,1:T(8,128)}) %reduce-scatter.25.cloned.1.call-update) | async-done | bytes 165904 | tf_op jit(solution)/shard_map/reduce_scatter | solution.py:230
  1074.9 61.2 %reduce-scatter.23.cloned.1.call-done = f32[144,3,288]{2,0,1:T(8,128)} async-done(((f32[1152,3,288]{2,0,1:T(8,128)}), f32[144,3,288]{2,0,1:T(8,128)}) %reduce-scatter.23.cloned.1.call-update) | async-done | bytes 497680 | tf_op jit(solution)/shard_map/reduce_scatter | solution.py:229
  1136.1 86.3 %reduce-scatter.21.cloned.1.call-done = f32[288,6,144]{0,2,1:T(8,128)} async-done(((f32[288,6,1152]{0,2,1:T(8,128)}), f32[288,6,144]{0,2,1:T(8,128)}) %reduce-scatter.21.cloned.1.call-update) | async-done | bytes 995344 | tf_op jit(solution)/shard_map/reduce_scatter | solution.py:228
  (248 shorter events, 110.9 us)
Async XLA Ops:
  7.2 3.6 copy-start.2
  7.2 46.9 %all-gather.10.cloned.1.call-start = ((), (), s32[]{:S(2)}) async-start(), calls=%async_computation.10 | async-start | bytes 5971968 | tf_op jit(solution)/shard_map/all_gather | solution.py:89
  7.9 46.1 %copy-start.34 = (bf16[1,288]{1,0:T(2,128)(2,1)S(1)}, bf16[1,288]{1,0:T(2,128)(2,1)}, u32[]{:S(2)}) copy-start(bf16[1,288]{1,0:T(2,128)(2,1)} %param.13) | copy-start | bytes 1732
  7.9 78.3 %all-gather.12.cloned.1.call-start = ((), (), s32[]{:S(2)}) async-start(), calls=%async_computation.11 | async-start | bytes 2985984 | tf_op jit(solution)/shard_map/all_gather | solution.py:90
  8.7 125.2 %all-gather.14.cloned.1.call-start = ((), (), s32[]{:S(2)}) async-start(), calls=%async_computation.12 | async-start | bytes 3538944 | tf_op jit(solution)/shard_map/all_gather | solution.py:116
  10.8 75.4 %copy-start.30 = (f32[1024]{0:T(1024)}, f32[1024]{0:T(1024)S(1)}, u32[]{:S(2)}) copy-start(f32[1024]{0:T(1024)S(1)} %broadcast_multiply_fusion) | copy-start | bytes 12292
  11.6 74.6 %copy-start.38 = (f32[1024]{0:T(1024)}, f32[1024]{0:T(1024)S(1)}, u32[]{:S(2)}) copy-start(f32[1024]{0:T(1024)S(1)} %add_rsqrt_fusion) | copy-start | bytes 12292
  77.5 13.3 %copy-start.22 = (f32[1152]{0:T(1024)}, f32[1152]{0:T(1024)S(1)}, u32[]{:S(2)}) copy-start(f32[1152]{0:T(1024)S(1)} %get-tuple-element.105) | copy-start | bytes 13828
  77.5 13.3 %copy-start.37 = (f32[1152]{0:T(1024)}, f32[1152]{0:T(1024)S(1)}, u32[]{:S(2)}) copy-start(f32[1152]{0:T(1024)S(1)} %get-tuple-element.104) | copy-start | bytes 13828
  93.1 25.5 %slice-start = ((bf16[1,1024,3,288]{1,3,2,0:T(8,128)(2,1)}), bf16[1,1024,1,288]{1,3,2,0:T(8,128)(2,1)S(1)}, s32[]{:S(2)}) async-start(bf16[1,1024,3,288]{1,3,2,0:T(8,128)(2,1)} %copy-done.11), calls=%async_computation.29 | async-start | bytes 1179648 | tf_op jit(solution)/shard_map/slice | solution.py:117
  93.1 173.3 %reduce-scatter.11.cloned.1.call-start = ((), (), s32[]{:S(2)}) async-start(), calls=%async_computation.13 | async-start | bytes 5898240 | tf_op jit(solution)/shard_map/reduce_scatter | solution.py:122
  175.5 5.4 copy-start
  181.0 117.9 %all-gather.18.cloned.1.call-start = ((), (), s32[]{:S(2)}) async-start(), calls=%async_computation.15 | async-start | bytes 2985984 | tf_op jit(solution)/shard_map/all_gather | solution.py:92
  181.6 169.9 %all-gather.16.cloned.1.call-start = ((), (), s32[]{:S(2)}) async-start(), calls=%async_computation.14 | async-start | bytes 2949120 | tf_op jit(solution)/shard_map/all_gather | solution.py:130
  187.2 81.8 %copy-start.32 = (f32[256]{0:T(256)}, f32[256]{0:T(256)S(1)}, u32[]{:S(2)}) copy-start(f32[256]{0:T(256)S(1)} %broadcast_multiply_fusion.1) | copy-start | bytes 3076
  270.3 112.1 %all-gather.20.cloned.1.call-start = ((), (), s32[]{:S(2)}) async-start(), calls=%async_computation.16 | async-start | bytes 2985984 | tf_op jit(solution)/shard_map/all_gather | solution.py:93
  271.1 212.5 %reduce-scatter.15.cloned.1.call-start = ((), (), s32[]{:S(2)}) async-start(), calls=%async_computation.19 | async-start | bytes 5898240 | tf_op jit(solution)/shard_map/reduce_scatter | solution.py:161
  382.4 10.5 copy-start.41
  398.1 136.9 %reduce-scatter.13.cloned.1.call-start = ((), (), s32[]{:S(2)}) async-start(), calls=%async_computation.17 | async-start | bytes 2949120 | tf_op jit(solution)/shard_map/reduce_scatter | solution.py:134
  407.0 185.2 %all-gather.24.cloned.1.call-start = ((), (), s32[]{:S(2)}) async-start(), calls=%async_computation.20 | async-start | bytes 2949120 | tf_op jit(solution)/shard_map/all_gather | solution.py:172
  535.0 2.8 copy-start.8
  535.0 2.8 copy-start.10
  542.0 170.2 %reduce-scatter.17.cloned.1.call-start = ((), (), s32[]{:S(2)}) async-start(), calls=%async_computation.21 | async-start | bytes 7077888 | tf_op jit(solution)/shard_map/reduce_scatter | solution.py:184
  542.5 56.4 %copy-start.1 = (bf16[4,1,1024,72]{3,2,1,0:T(8,128)(2,1)S(1)}, bf16[4,1,1024,72]{3,2,1,0:T(8,128)(2,1)}, u32[]{:S(2)}) copy-start(bf16[4,1,1024,72]{3,2,1,0:T(8,128)(2,1)} %copy-done) | copy-start | bytes 1769476
  605.9 2.2 copy-start.16
  618.2 2.2 copy-start.16
  630.5 2.2 copy-start.16
  642.8 2.2 copy-start.16
  653.2 61.8 %copy-start.18 = (bf16[4,1,1024,72]{2,3,1,0:T(8,128)(2,1)S(1)}, bf16[4,1,1024,72]{2,3,1,0:T(8,128)(2,1)}, u32[]{:S(2)}) copy-start(bf16[4,1,1024,72]{2,3,1,0:T(8,128)(2,1)} %get-tuple-element.92) | copy-start | bytes 1769476
  653.2 61.8 %copy-start.40 = (bf16[1152,3,288]{2,0,1:T(8,128)(2,1)S(1)}, bf16[1152,3,288]{2,0,1:T(8,128)(2,1)}, u32[]{:S(2)}) copy-start(bf16[1152,3,288]{2,0,1:T(8,128)(2,1)} %all-gather.12.cloned.1.call-done) | copy-start | bytes 5971972
  653.2 152.6 %reduce-scatter.19.cloned.1.call-start = ((), (), s32[]{:S(2)}) async-start(), calls=%async_computation.22 | async-start | bytes 5898240 | tf_op jit(solution)/shard_map/reduce_scatter | solution.py:189
  720.4 85.5 %copy-start.23 = (f32[1152]{0:T(1024)S(1)}, f32[1152]{0:T(1024)}, u32[]{:S(2)}) copy-start(f32[1152]{0:T(1024)} %copy-done.22) | copy-start | bytes 13828
  720.4 85.5 %copy-start.33 = (f32[256]{0:T(256)S(1)}, f32[256]{0:T(256)}, u32[]{:S(2)}) copy-start(f32[256]{0:T(256)} %copy-done.32) | copy-start | bytes 3076
  720.4 165.1 %all-gather.22.cloned.1.call-start = ((), (), s32[]{:S(2)}) async-start(), calls=%async_computation.18 | async-start | bytes 2949120 | tf_op jit(solution)/shard_map/all_gather | solution.py:202
  721.1 189.4 %all-gather.26.cloned.1.call-start = ((), (), s32[]{:S(2)}) async-start(), calls=%async_computation.23 | async-start | bytes 2949120 | tf_op jit(solution)/shard_map/all_gather | solution.py:203
  721.2 89.1 %copy-start.6 = (f32[1,256,1152]{2,1,0:T(8,128)S(1)}, f32[1,256,1152]{2,1,0:T(8,128)}, u32[]{:S(2)}) copy-start(f32[1,256,1152]{2,1,0:T(8,128)} %copy-done.5) | copy-start | bytes 3538948
  805.8 2.7 copy-start.7
  811.3 159.2 %reduce-scatter.29.cloned.1.call-start = ((), (), s32[]{:S(2)}) async-start(), calls=%async_computation.28 | async-start | bytes 5971968 | tf_op jit(solution)/shard_map/reduce_scatter | solution.py:232
  820.2 211.1 %reduce-scatter.27.cloned.1.call-start = ((), (), s32[]{:S(2)}) async-start(), calls=%async_computation.27 | async-start | bytes 5971968 | tf_op jit(solution)/shard_map/reduce_scatter | solution.py:231
  829.2 4.8 copy-start.3
  829.2 4.8 copy-start.15
  829.2 4.8 copy-start.31
  829.2 4.8 copy-start.39
  829.2 245.7 %reduce-scatter.25.cloned.1.call-start = ((), (), s32[]{:S(2)}) async-start(), calls=%async_computation.26 | async-start | bytes 1990656 | tf_op jit(solution)/shard_map/reduce_scatter | solution.py:230
  834.0 302.1 %reduce-scatter.23.cloned.1.call-start = ((), (), s32[]{:S(2)}) async-start(), calls=%async_computation.25 | async-start | bytes 5971968 | tf_op jit(solution)/shard_map/reduce_scatter | solution.py:229
  841.3 381.1 %reduce-scatter.21.cloned.1.call-start = ((), (), s32[]{:S(2)}) async-start(), calls=%async_computation.24 | async-start | bytes 11943936 | tf_op jit(solution)/shard_map/reduce_scatter | solution.py:228
  885.5 337.0 %copy-start.12 = (bf16[1,1024,1152]{2,1,0:T(8,128)(2,1)S(1)}, bf16[1,1024,1152]{2,1,0:T(8,128)(2,1)}, u32[]{:S(2)}) copy-start(bf16[1,1024,1152]{2,1,0:T(8,128)(2,1)} %all-gather.22.cloned.1.call-done) | copy-start | bytes 7077892
  1222.4 2.5 copy-start.13
  (31 other events, 38.5 us)
Sparse Core Ops, SparseCore 0:
  9.9 44.0 all-gather.9
  55.9 30.2 all-gather.11
  93.2 40.6 all-gather.13
  181.1 85.2 reduce-scatter.10
  268.1 30.7 all-gather.17
  300.9 50.4 all-gather.15
  353.3 29.0 all-gather.19
  398.2 85.2 reduce-scatter.14
  486.4 48.5 reduce-scatter.12
  542.1 49.9 all-gather.23
  653.3 58.8 reduce-scatter.16
  720.5 85.2 reduce-scatter.18
  807.5 51.9 all-gather.21
  860.9 49.5 all-gather.25
  914.7 55.7 reduce-scatter.28
  974.4 56.9 reduce-scatter.26
  1035.5 39.3 reduce-scatter.24
  1079.1 56.9 reduce-scatter.22
  1140.2 82.1 reduce-scatter.20
where the time goes:
time: 1240 us; the launch traced here: 1230 us
  waiting for transfers between devices  898 us (72%)
  matrix products  147 us (12%)
  blocking collectives  83.6 us (7%)
  other arithmetic  57.9 us (5%)
  local copies, waits for them, and re-layouts  30.1 us (2%)
  between operations  14.8 us (1%)
    reduce_scatter x1, waiting for transfers between devices, shards(): lax.psum_scatter(grad_modulation, ('fsdp', 'ctx'), scatter_dimension=2, t...  86.3 us
    reduce_scatter x1, waiting for transfers between devices, shards(): lax.psum_scatter(jnp.einsum('btkc,dkc->btd', grad_projected, qkv_back, pr...  84.6 us
    reduce_scatter x1, waiting for transfers between devices, shards(): lax.psum_scatter(jnp.einsum('btc,cd->btd', attended, out_full, preferred_...  79.2 us
    reduce_scatter x1, waiting for transfers between devices, shards(): lax.psum_scatter(jnp.einsum('btf,df->btd', grad_pre, expand_back, preferr...  72.4 us
    reduce_scatter x1, waiting for transfers between devices, shards(): lax.psum_scatter(grad_attention, ('fsdp', 'ctx'), scatter_dimension=0, ti...  61.2 us
    reduce_scatter x1, waiting for transfers between devices, shards(): lax.psum_scatter(grad_expand, ('fsdp', 'ctx'), scatter_dimension=0, tiled...  60.8 us
    reduce_scatter x1, waiting for transfers between devices, shards(): lax.psum_scatter(grad_contract, ('fsdp', 'ctx'), scatter_dimension=1, til...  60 us
    reduce_scatter x1, waiting for transfers between devices, shards(): lax.psum_scatter(pair_terms, 'ctx', scatter_dimension=1, tiled=True)  58.9 us
  transfers between devices with their start and end apart: 19, of which 18 were waited for; matrix products, arithmetic and copies ran while one was open for 7% of the time, Pallas kernels for 0%

commit v1 on v0

--- a/solution.py
+++ b/solution.py
@@ -85,21 +85,31 @@
     contract_weight,
     cotangent,
 ):
-    ada_full, qkv_full, out_full, expand_full, contract_full = (
-        lax.all_gather(modulation_weight, ("fsdp", "ctx"), axis=2, tiled=True),
-        lax.all_gather(attention_weight, ("fsdp", "ctx"), axis=0, tiled=True),
-        lax.all_gather(output_weight, ("fsdp", "ctx"), axis=1, tiled=True),
-        lax.all_gather(expand_weight, ("fsdp", "ctx"), axis=0, tiled=True),
-        lax.all_gather(contract_weight, ("fsdp", "ctx"), axis=1, tiled=True),
-    )
+    everywhere = ("fsdp", "ctx")
+    qkv_full = lax.all_gather(attention_weight, everywhere, axis=0, tiled=True)
+    ff_part = expand_weight.shape[1]
+    rest = jnp.concatenate((output_weight.T, expand_weight, contract_weight.T), axis=1)
+    rest_full = lax.all_gather(rest, everywhere, axis=0, tiled=True)
+    head_part = output_weight.shape[0]
+    out_t = rest_full[:, :head_part]
+    expand_full = rest_full[:, head_part : head_part + ff_part]
+    contract_t = rest_full[:, head_part + ff_part :]
+    own_latent = lax.axis_index("fsdp")
     share_rows = latents.shape[1] // lax.axis_size("tp")
     share_start = lax.axis_index("tp") * share_rows
     cond_float = conditioning.astype(jnp.float32)
     cond_silu, silu_pull = jax.vjp(jax.nn.silu, cond_float)
     cond_act = cond_silu.astype(jnp.bfloat16)
-    modulations = lax.psum(
-        jnp.einsum("bd,dkc->bkc", cond_act, ada_full, preferred_element_type=jnp.float32), "tp"
-    )
+    cond_all = lax.all_gather(cond_act, "fsdp", axis=0, tiled=True)
+    mod_terms = jnp.einsum(
+        "bd,dkc->bkc", cond_all, modulation_weight, preferred_element_type=jnp.float32
+    )
+    mod_parts = lax.all_gather(mod_terms, ("tp", "fsdp", "ctx"), axis=0)
+    mod_parts = lax.dynamic_slice_in_dim(mod_parts, own_latent, 1, 1)
+    column_parts = mod_parts.shape[0] // lax.axis_size("tp")
+    mod_parts = mod_parts.reshape((lax.axis_size("tp"), column_parts) + mod_parts.shape[2:])
+    modulations = jnp.sum(mod_parts, axis=0).transpose(1, 0, 2)
+    modulations = modulations.reshape(1, modulations.shape[0], -1)
     shift_one = modulations[:, 0]
     scale_one = modulations[:, 1]
     gate_one = modulations[:, 2]
@@ -120,11 +130,13 @@
     mixed_values, logsum = lax.map(forward_head, (heads_query, keys_heads, values_heads))
     attended = token_major(mixed_values).astype(jnp.bfloat16)
     branch_one = lax.psum_scatter(
-        jnp.einsum("btc,cd->btd", attended, out_full, preferred_element_type=jnp.float32),
-        "tp",
-        scatter_dimension=1,
-        tiled=True,
-    )
+        jnp.einsum(
+            "btc,dc->btd", attended, out_t, preferred_element_type=jnp.float32
+        ).astype(jnp.bfloat16),
+        "tp",
+        scatter_dimension=1,
+        tiled=True,
+    ).astype(jnp.float32)
     hidden = token_share + gate_one[:, None, :] * branch_one
     normed_two, norm_pull_two = jax.vjp(modulate, hidden, shift_two, scale_two)
     act_two = lax.all_gather(normed_two.astype(jnp.bfloat16), "tp", axis=1, tiled=True)
@@ -133,37 +145,32 @@
     activated = gelu_value.astype(jnp.bfloat16)
     branch_two = lax.psum_scatter(
         jnp.einsum(
-            "btf,fd->btd", activated, contract_full, preferred_element_type=jnp.float32
+            "btf,df->btd", activated, contract_t, preferred_element_type=jnp.float32
         ).astype(jnp.bfloat16),
         "tp",
         scatter_dimension=1,
         tiled=True,
     ).astype(jnp.float32)
     block_share = (hidden + gate_two[:, None, :] * branch_two).astype(jnp.bfloat16)
-    ada_back, qkv_back, out_back, expand_back, contract_back = (
-        lax.all_gather(modulation_weight, ("fsdp", "ctx"), axis=2, tiled=True),
-        lax.all_gather(attention_weight, ("fsdp", "ctx"), axis=0, tiled=True),
-        lax.all_gather(output_weight, ("fsdp", "ctx"), axis=1, tiled=True),
-        lax.all_gather(expand_weight, ("fsdp", "ctx"), axis=0, tiled=True),
-        lax.all_gather(contract_weight, ("fsdp", "ctx"), axis=1, tiled=True),
-    )
     grad_out_full = cotangent.astype(jnp.float32)
     grad_out = lax.dynamic_slice_in_dim(grad_out_full, share_start, share_rows, 1)
     grad_gate_two = jnp.sum(grad_out * branch_two, axis=1)
     grad_branch_two = (grad_out_full * gate_two[:, None, :]).astype(jnp.bfloat16)
     grad_activated = jnp.einsum(
-        "btd,fd->btf", grad_branch_two, contract_back, preferred_element_type=jnp.float32
+        "btd,df->btf", grad_branch_two, contract_t, preferred_element_type=jnp.float32
     )
     grad_pre = gelu_pull(grad_activated)[0].astype(jnp.bfloat16)
     grad_contract = jnp.einsum(
-        "btf,btd->fd", activated, grad_branch_two, preferred_element_type=jnp.float32
+        "btd,btf->df", grad_branch_two, activated, preferred_element_type=jnp.float32
     )
     grad_act_two = lax.psum_scatter(
-        jnp.einsum("btf,df->btd", grad_pre, expand_back, preferred_element_type=jnp.float32),
-        "tp",
-        scatter_dimension=1,
-        tiled=True,
-    )
+        jnp.einsum(
+            "btf,df->btd", grad_pre, expand_full, preferred_element_type=jnp.float32
+        ).astype(jnp.bfloat16),
+        "tp",
+        scatter_dimension=1,
+        tiled=True,
+    ).astype(jnp.float32)
     grad_expand = jnp.einsum("btd,btf->df", act_two, grad_pre, preferred_element_type=jnp.float32)
     grad_hidden, grad_shift_two, grad_scale_two = norm_pull_two(grad_act_two)
     grad_hidden = grad_hidden + grad_out
@@ -171,27 +178,34 @@
     branch_grad_share = (grad_hidden * gate_one[:, None, :]).astype(jnp.bfloat16)
     grad_branch_one = lax.all_gather(branch_grad_share, "tp", axis=1, tiled=True)
     grad_attended = jnp.einsum(
-        "btd,cd->btc", grad_branch_one, out_back, preferred_element_type=jnp.float32
+        "btd,dc->btc", grad_branch_one, out_t, preferred_element_type=jnp.float32
     ).astype(jnp.bfloat16)
     grad_output = jnp.einsum(
-        "btc,btd->cd", attended, grad_branch_one, preferred_element_type=jnp.float32
-    )
+        "btd,btc->dc", grad_branch_one, attended, preferred_element_type=jnp.float32
+    )
+    grad_rest = jnp.concatenate((grad_output, grad_expand, grad_contract), axis=1)
+    grad_rest = lax.psum_scatter(
+        grad_rest.astype(jnp.bfloat16), everywhere, scatter_dimension=0, tiled=True
+    ).astype(jnp.float32)
     heads_grad = head_major(grad_attended)
     grads_query, grads_keys, grads_values = lax.map(
         backward_head, (heads_query, keys_heads, values_heads, heads_grad, logsum)
     )
     pair_terms = jnp.stack((token_major(grads_keys), token_major(grads_values)), axis=2)
+    pair_terms = pair_terms.astype(jnp.bfloat16)
     grad_pair = lax.psum_scatter(pair_terms, "ctx", scatter_dimension=1, tiled=True).astype(
         jnp.bfloat16
     )
     grad_query = token_major(grads_query).astype(jnp.bfloat16)
     grad_projected = jnp.concatenate((grad_query[:, :, None], grad_pair), axis=2)
     grad_act_one = lax.psum_scatter(
-        jnp.einsum("btkc,dkc->btd", grad_projected, qkv_back, preferred_element_type=jnp.float32),
-        "tp",
-        scatter_dimension=1,
-        tiled=True,
-    )
+        jnp.einsum(
+            "btkc,dkc->btd", grad_projected, qkv_full, preferred_element_type=jnp.float32
+        ).astype(jnp.bfloat16),
+        "tp",
+        scatter_dimension=1,
+        tiled=True,
+    ).astype(jnp.float32)
     grad_attention = jnp.einsum(
         "btd,btkc->dkc", act_one, grad_projected, preferred_element_type=jnp.float32
     )
@@ -213,33 +227,36 @@
         ),
         axis=1,
     )
-    grad_modulations = lax.psum(grad_parts, ("ctx", "tp"))
+    grad_attention = lax.psum_scatter(
+        grad_attention.astype(jnp.bfloat16), everywhere, scatter_dimension=0, tiled=True
+    ).astype(jnp.float32)
+    grad_modulations = lax.all_gather(grad_parts[0], ("ctx", "tp", "fsdp"), axis=0)
+    latent_count = lax.axis_size("fsdp")
+    grad_modulations = jnp.sum(
+        grad_modulations.reshape((-1, latent_count) + grad_modulations.shape[1:]), axis=0
+    )
+    column_count = modulation_weight.shape[2]
+    column_start = lax.axis_index(everywhere) * column_count
+    grad_columns = lax.dynamic_slice_in_dim(grad_modulations, column_start, column_count, 2)
     grad_modulation = jnp.einsum(
-        "bd,bkc->dkc", cond_act.astype(jnp.float32), grad_modulations, precision=highest
-    )
-    grad_modulation = jnp.where(
-        lax.axis_index("ctx") == 0, grad_modulation, jnp.zeros_like(grad_modulation)
-    )
-    grad_cond_act = jnp.einsum(
-        "bkc,dkc->bd", grad_modulations, ada_back.astype(jnp.float32), precision=highest
+        "bd,bkc->dkc", cond_all.astype(jnp.float32), grad_columns, precision=highest
+    )
+    grad_cond_terms = jnp.einsum(
+        "bkc,dkc->bd", grad_columns, modulation_weight.astype(jnp.float32), precision=highest
+    )
+    grad_cond_act = lax.dynamic_slice_in_dim(
+        lax.psum(grad_cond_terms, everywhere), own_latent, 1, 0
     )
     conditioning_grad = silu_pull(grad_cond_act)[0]
-    summed = (
-        lax.psum_scatter(grad_modulation, ("fsdp", "ctx"), scatter_dimension=2, tiled=True),
-        lax.psum_scatter(grad_attention, ("fsdp", "ctx"), scatter_dimension=0, tiled=True),
-        lax.psum_scatter(grad_output, ("fsdp", "ctx"), scatter_dimension=1, tiled=True),
-        lax.psum_scatter(grad_expand, ("fsdp", "ctx"), scatter_dimension=0, tiled=True),
-        lax.psum_scatter(grad_contract, ("fsdp", "ctx"), scatter_dimension=1, tiled=True),
-    )
     return (
         block_out,
         latents_grad,
         conditioning_grad,
-        summed[0],
-        summed[1],
-        summed[2],
-        summed[3],
-        summed[4],
+        grad_modulation,
+        grad_attention,
+        grad_rest[:, :head_part].T,
+        grad_rest[:, head_part : head_part + ff_part],
+        grad_rest[:, head_part + ff_part :].T,
     )
 
 

time: 1240 us -> 876 us (0.71)
  waiting for transfers between devices: 898 us -> 462 us
  blocking collectives: 83.6 us -> 146 us
  local copies, waits for them, and re-layouts: 30.1 us -> 44 us
    reduce_scatter x9 -> x5, waiting for transfers between devices: 597 us -> 183 us  [the longest x1 46.3 us: shards(): lax.psum_scatter(grad_attention.astype(jnp.bfloat16), everywhere, scatter...]
    all_gather x1 -> x3, blocking collectives: 25.4 us -> 133 us  [the longest x1 75.3 us: shards(): mod_parts = lax.all_gather(mod_terms, ('tp', 'fsdp', 'ctx'), axis=0)]
    all_gather x4 -> x2, waiting for transfers between devices: 102 us -> 6.18 us  [the longest x1 6.16 us: shards(): rest_full = lax.all_gather(rest, everywhere, axis=0, tiled=True)]
    unnamed x19 -> x15, waiting for transfers between devices: 3.53 us -> 65.1 us
    all_gather x1, waiting for transfers between devices: 0.02 us -> 45.4 us  [shards(): lax.all_gather(block_share, 'tp', axis=1, tiled=True)]
    psum x2 -> x1, blocking collectives: 58.1 us -> 13.5 us  [shards(): lax.psum(grad_cond_terms, everywhere)]
    reduce_scatter x1, waiting for transfers between devices: 58.9 us -> 33.2 us  [shards(): lax.psum_scatter(pair_terms, 'ctx', scatter_dimension=1, tiled=True)]
    all_gather x1, waiting for transfers between devices: 19.6 us -> 0.01 us  [shards(): lax.all_gather(grad_tokens.astype(jnp.bfloat16), 'tp', axis=1, tiled=True)]
  transfers between devices with their start and end apart: 19 -> 14, of which waited for: 18 -> 12; matrix products, arithmetic and copies ran while one was open for 7% -> 14% of each run, Pallas kernels for 0% -> 0%
where the time goes in v1:
time: 876 us; the launch traced here: 867 us
  waiting for transfers between devices  462 us (53%)
  blocking collectives  146 us (17%)
  matrix products  141 us (16%)
  other arithmetic  56 us (6%)
  local copies, waits for them, and re-layouts  44 us (5%)
  between operations  14.8 us (2%)
    all_gather x1, blocking collectives, shards(): mod_parts = lax.all_gather(mod_terms, ('tp', 'fsdp', 'ctx'), axis=0)  75.3 us
    unnamed x15, waiting for transfers between devices  65.1 us
    all_gather x1, blocking collectives, shards(): lax.all_gather(grad_parts[0], ('ctx', 'tp', 'fsdp'), axis=0)  51.4 us
    all_gather x1, waiting for transfers between devices, shards(): lax.all_gather(normed_two.astype(jnp.bfloat16), 'tp', axis=1, tiled=True)  50.1 us
    all_gather x1, waiting for transfers between devices, shards(): lax.all_gather(branch_grad_share, 'tp', axis=1, tiled=True)  49.9 us
    reduce_scatter x1, waiting for transfers between devices, shards(): lax.psum_scatter(grad_attention.astype(jnp.bfloat16), everywhere, scatter...  46.3 us
    reduce_scatter x1, waiting for transfers between devices, shards(): lax.psum_scatter(jnp.einsum('btf,df->btd', activated, contract_t, preferr...  46.3 us
    all_gather x1, waiting for transfers between devices, shards(): lax.all_gather(block_share, 'tp', axis=1, tiled=True)  45.4 us
  transfers between devices with their start and end apart: 14, of which 12 were waited for; matrix products, arithmetic and copies ran while one was open for 14% of the time, Pallas kernels for 0%

profile of v1, /device:TPU:0, one launch (start us, length us, event | category | flops | bytes accessed | tf_op | source)
XLA Modules:
  0.0 866.6 jit_solution(9366923385377719569)
XLA Ops:
  9.3 6.1 all-gather.1
  16.4 75.3 %all-gather = f32[128,6,144]{2,1,0:T(8,128)S(1)} all-gather(f32[4,6,144]{2,1,0:T(8,128)S(1)} %copy.52), channel_id=2, replica_groups=mesh['fsdp'=4,'ctx'=2,'tp'=4] {'tp','fsdp','ctx'}, dimensions={0}, use_global_device_ids=true | all-gather | bytes 456192 | tf_op jit(solution)/shard_map/all_gather | solution.py:107
  93.2 4.6 convert_bitcast_fusion
  103.3 29.0 %all-gather.12.cloned.1.call-done = bf16[1,2048,2,288]{1,3,2,0:T(8,128)(2,1)} async-done(((bf16[1,1024,2,288]{1,3,2,0:T(8,128)(2,1)}), bf16[1,2048,2,288]{1,3,2,0:T(8,128)(2,1)}) %all-gather.12.cloned.1.call-update) | async-done | bytes 2359312 | tf_op jit(solution)/shard_map/all_gather | solution.py:126
  132.3 3.3 fusion.117
  135.6 2.8 copy.55
  138.5 3.6 copy.56
  142.1 31.6 %while.26 = (s32[]{:T(128)}, bf16[4,1,1024,72]{2,3,1,0:T(8,128)(2,1)S(1)}, f32[4,1,1024]{2,1,0:T(1,128)S(1)}, bf16[4,1,1024,72]{3,2,1,0:T(8,128)(2,1)}, bf16[4,1...) while((s32[]{:T(128)}, bf16[4,1,1024,72]{2,3,1,0:T(8,128)(2,1)S(1)}, ...), condition=%wide.region_6.7_spmd, body=%wide.region_3.6_spmd.sunk | while | flops 622853120 | bytes 26814544 | solution.py:130
  146.4 3.6 fusion.145
  154.3 3.6 fusion.145
  162.2 3.6 fusion.145
  170.1 3.6 fusion.145
  173.8 6.2 all-gather.14.cloned.1.call-done
  179.9 4.1 fusion.56
  184.6 4.1 convert_element_type.150
  188.7 43.6 %reduce-scatter.10.cloned.1.call-done = bf16[1,256,1152]{2,1,0:T(8,128)(2,1)} async-done(((bf16[1,1024,1152]{2,1,0:T(8,128)(2,1)}), bf16[1,256,1152]{2,1,0:T(8,128)(2,1)}) %reduce-scatter.10.cloned.1.call-update) | async-done | bytes 589840 | tf_op jit(solution)/shard_map/reduce_scatter | solution.py:132
  236.8 50.1 %all-gather.16.cloned.1.call-done = bf16[1,1024,1152]{2,1,0:T(8,128)(2,1)} async-done(((bf16[1,256,1152]{2,1,0:T(8,128)(2,1)}), bf16[1,1024,1152]{2,1,0:T(8,128)(2,1)}) %all-gather.16.cloned.1.call-update) | async-done | bytes 2359312 | tf_op jit(solution)/shard_map/all_gather | solution.py:142
  286.9 6.3 fusion.66
  293.2 9.4 %fusion.55 = bf16[1024,1152]{1,0:T(8,128)(2,1)S(1)} fusion(f32[1024,1152]{1,0:T(8,128)S(1)} %fusion.66, bf16[1152,2592]{1,0:T(8,128)(2,1)} %all-gather.14.cloned.1.call-done, f32[1152]{0:T(1024)S(1)} %get-tuple-element.143, bf16[1,1024,1152]{2,1,0:T(8,128)(2,1)S(1)} %copy-done.11), kind=kOutput, calls=%fused_computation.66 | convolution fusion | flops 2745040896 | bytes 12096000 | tf_op jit(solution)/shard_map/btd,df->btf/dot_general | solution.py:159
  304.0 6.9 fusion.59
  311.2 9.1 %fusion.58 = bf16[1,1024,1152]{2,1,0:T(8,128)(2,1)} fusion(bf16[1152,2592]{1,0:T(8,128)(2,1)} %all-gather.14.cloned.1.call-done, f32[1024,1152]{1,0:T(8,128)} %copy-done.41), kind=kOutput, calls=%fused_computation.79 | convolution fusion | flops 2729705472 | bytes 9732096 | tf_op jit(solution)/shard_map/btf,df->btd/dot_general | solution.py:147
  320.3 4.1 convert_element_type.168
  324.4 33.5 %reduce-scatter.14.cloned.1.call-done = bf16[1,256,1152]{2,1,0:T(8,128)(2,1)} async-done(((bf16[1,1024,1152]{2,1,0:T(8,128)(2,1)}), bf16[1,256,1152]{2,1,0:T(8,128)(2,1)}) %reduce-scatter.14.cloned.1.call-update) | async-done | bytes 589840 | tf_op jit(solution)/shard_map/reduce_scatter | solution.py:166
  362.1 46.3 %reduce-scatter.12.cloned.1.call-done = bf16[1,256,1152]{2,1,0:T(8,128)(2,1)} async-done(((bf16[1,1024,1152]{2,1,0:T(8,128)(2,1)}), bf16[1,256,1152]{2,1,0:T(8,128)(2,1)}) %reduce-scatter.12.cloned.1.call-update) | async-done | bytes 589840 | tf_op jit(solution)/shard_map/reduce_scatter | solution.py:146
  408.4 4.2 fusion.85
  414.8 49.9 %all-gather.20.cloned.1.call-done = bf16[1,1024,1152]{2,1,0:T(8,128)(2,1)} async-done(((bf16[1,256,1152]{2,1,0:T(8,128)(2,1)}), bf16[1,1024,1152]{2,1,0:T(8,128)(2,1)}) %all-gather.20.cloned.1.call-update) | async-done | bytes 2359312 | tf_op jit(solution)/shard_map/all_gather | solution.py:179
  464.6 2.8 fusion.79
  468.8 53.7 %while.27 = (s32[]{:T(128)}, bf16[4,1,1024,72]{2,3,1,0:T(8,128)(2,1)S(1)}, bf16[4,1,2048,72]{2,3,1,0:T(8,128)(2,1)}, bf16[4,1,2048,72]{2,3,1,0:T(8,128)(2,1)}, b...) while((s32[]{:T(128)}, ...), condition=%wide.region_16.17_spmd, body=%wide.region_14.16_spmd.sunk | while | flops 1535335424 | bytes 78841024 | solution.py:191
  471.2 3.2 multiply_reduce_fusion.8
  484.6 3.2 multiply_reduce_fusion.8
  498.0 3.2 multiply_reduce_fusion.8
  511.4 3.2 multiply_reduce_fusion.8
  522.5 3.5 pad_maximum_fusion.1
  526.5 33.2 %reduce-scatter.16.cloned.1.call-done = bf16[1,1024,2,288]{1,3,2,0:T(8,128)(2,1)} async-done(((bf16[1,2048,2,288]{1,3,2,0:T(8,128)(2,1)}), bf16[1,1024,2,288]{1,3,2,0:T(8,128)(2,1)}) %reduce-scatter.16.cloned.1.call-update) | async-done | bytes 1179664 | tf_op jit(solution)/shard_map/reduce_scatter | solution.py:196
  559.7 7.2 fusion.57
  568.5 6.8 convolution_convert_fusion.2
  575.6 5.8 convolution_convert_fusion.1
  581.4 6.6 convolution_convert_fusion
  588.9 3.1 pad_maximum_fusion
  592.0 9.3 %copy.66 = bf16[1152,2592]{1,0:T(8,128)(2,1)} copy(bf16[1152,2592]{0,1:T(8,128)(2,1)} %pad_maximum_fusion) | data formatting | bytes 11943936
  602.0 13.1 %reduce-scatter.18.cloned.1.call-done = bf16[1,256,1152]{2,1,0:T(8,128)(2,1)} async-done(((bf16[1,1024,1152]{2,1,0:T(8,128)(2,1)}), bf16[1,256,1152]{2,1,0:T(8,128)(2,1)}) %reduce-scatter.18.cloned.1.call-update) | async-done | bytes 589840 | tf_op jit(solution)/shard_map/reduce_scatter | solution.py:201
  619.2 2.6 add_convert_fusion.1
  621.9 45.4 %all-gather.18.cloned.1.call-done = bf16[1,1024,1152]{2,1,0:T(8,128)(2,1)} async-done(((bf16[1,256,1152]{2,1,0:T(8,128)(2,1)}), bf16[1,1024,1152]{2,1,0:T(8,128)(2,1)}) %all-gather.18.cloned.1.call-update) | async-done | bytes 2359312 | tf_op jit(solution)/shard_map/all_gather | solution.py:216
  667.4 46.3 %reduce-scatter.20.cloned.1.call-done = bf16[144,3,288]{2,0,1:T(8,128)(2,1)} async-done(((bf16[1152,3,288]{2,0,1:T(8,128)(2,1)}), bf16[144,3,288]{2,0,1:T(8,128)(2,1)}) %reduce-scatter.20.cloned.1.call-update) | async-done | bytes 248848 | tf_op jit(solution)/shard_map/reduce_scatter | solution.py:230
  715.6 63.5 %reduce-scatter.22.cloned.1.call-done = bf16[144,2592]{1,0:T(8,128)(2,1)} async-done(((bf16[1152,2592]{1,0:T(8,128)(2,1)}), bf16[144,2592]{1,0:T(8,128)(2,1)}) %reduce-scatter.22.cloned.1.call-update) | async-done | bytes 746512
  787.2 51.4 %all_gather.43 = f32[32,6,1152]{2,1,0:T(8,128)S(1)} all-gather(f32[1,6,1152]{2,1,0:T(8,128)S(1)} %stack.21), channel_id=1, replica_groups=mesh['fsdp'=4,'ctx'=2,'tp'=4] {'ctx','tp','fsdp'}, dimensions={0}, use_global_device_ids=true | all-gather | bytes 912384 | tf_op jit(solution)/shard_map/all_gather | solution.py:233
  839.1 13.5 %psum.7 = f32[4,288]{1,0:T(4,128)S(1)} all-reduce(f32[4,288]{1,0:T(4,128)S(1)} %convolution_bitcast_fusion), channel_id=1, replica_groups=mesh['fsdp'=4,'ctx'=2,'tp'=4] {'fsdp','ctx'}, use_global_device_ids=true, to_apply=%region_30.31 | all-reduce | flops 1152 | bytes 9216 | tf_op jit(solution)/shard_map/psum | solution.py:248
  855.0 3.4 copy.119
  (235 shorter events, 104.0 us)
Async XLA Ops:
  7.2 8.8 %copy-start = (bf16[288,6,144]{0,2,1:T(8,128)(2,1)S(1)}, bf16[288,6,144]{0,2,1:T(8,128)(2,1)}, u32[]{:S(2)}) copy-start(bf16[288,6,144]{0,2,1:T(8,128)(2,1)} %param.14) | copy-start | bytes 1492996
  7.2 84.8 %copy-start.3 = (bf16[1,1024,1152]{2,1,0:T(8,128)(2,1)S(1)}, bf16[1,1024,1152]{2,1,0:T(8,128)(2,1)}, u32[]{:S(2)}) copy-start(bf16[1,1024,1152]{2,1,0:T(8,128)(2,1)} %param.12) | copy-start | bytes 7077892
  7.2 86.0 %all-gather.10.cloned.1.call-start = ((), (), s32[]{:S(2)}) async-start(), calls=%async_computation.7 | async-start | bytes 2985984 | tf_op jit(solution)/shard_map/all_gather | solution.py:89
  7.9 124.4 %all-gather.12.cloned.1.call-start = ((), (), s32[]{:S(2)}) async-start(), calls=%async_computation.8 | async-start | bytes 3538944 | tf_op jit(solution)/shard_map/all_gather | solution.py:126
  92.4 5.5 copy-start.31
  93.1 4.7 copy-start.38
  100.2 1.8 slice-start
  100.2 79.7 %all-gather.14.cloned.1.call-start = ((), (), s32[]{:S(2)}) async-start(), calls=%async_computation.9 | async-start | bytes 6967296 | tf_op jit(solution)/shard_map/all_gather | solution.py:92
  101.9 130.4 %reduce-scatter.10.cloned.1.call-start = ((), (), s32[]{:S(2)}) async-start(), calls=%async_computation.10 | async-start | bytes 2949120 | tf_op jit(solution)/shard_map/reduce_scatter | solution.py:132
  173.7 10.3 %copy-start.18 = (bf16[4,1,1024,72]{2,3,1,0:T(8,128)(2,1)}, bf16[4,1,1024,72]{2,3,1,0:T(8,128)(2,1)S(1)}, u32[]{:S(2)}) copy-start(bf16[4,1,1024,72]{2,3,1,0:T(8,128)(2,1)S(1)} %get-tuple-element.90) | copy-start | bytes 1769476
  184.0 102.8 %all-gather.16.cloned.1.call-start = ((), (), s32[]{:S(2)}) async-start(), calls=%async_computation.11 | async-start | bytes 2949120 | tf_op jit(solution)/shard_map/all_gather | solution.py:142
  236.7 121.2 %reduce-scatter.14.cloned.1.call-start = ((), (), s32[]{:S(2)}) async-start(), calls=%async_computation.14 | async-start | bytes 2949120 | tf_op jit(solution)/shard_map/reduce_scatter | solution.py:166
  286.9 6.3 copy-start.11
  293.2 9.5 %copy-start.41 = (f32[1024,1152]{1,0:T(8,128)}, f32[1024,1152]{1,0:T(8,128)S(1)}, u32[]{:S(2)}) copy-start(f32[1024,1152]{1,0:T(8,128)S(1)} %fusion.66) | copy-start | bytes 14155780
  311.0 97.4 %reduce-scatter.12.cloned.1.call-start = ((), (), s32[]{:S(2)}) async-start(), calls=%async_computation.12 | async-start | bytes 2949120 | tf_op jit(solution)/shard_map/reduce_scatter | solution.py:146
  320.3 144.3 %all-gather.20.cloned.1.call-start = ((), (), s32[]{:S(2)}) async-start(), calls=%async_computation.15 | async-start | bytes 2949120 | tf_op jit(solution)/shard_map/all_gather | solution.py:179
  357.9 1.9 copy-start.2
  357.9 50.4 %copy-start.9 = (bf16[1,256,1152]{2,1,0:T(8,128)(2,1)S(1)}, bf16[1,256,1152]{2,1,0:T(8,128)(2,1)}, u32[]{:S(2)}) copy-start(bf16[1,256,1152]{2,1,0:T(8,128)(2,1)} %reduce-scatter.14.cloned.1.call-done) | copy-start | bytes 1769476
  414.5 145.2 %reduce-scatter.16.cloned.1.call-start = ((), (), s32[]{:S(2)}) async-start(), calls=%async_computation.16 | async-start | bytes 3538944 | tf_op jit(solution)/shard_map/reduce_scatter | solution.py:196
  468.9 2.3 copy-start.5
  474.4 2.2 copy-start.15
  482.3 2.3 copy-start.5
  487.8 2.2 copy-start.15
  495.7 2.3 copy-start.5
  501.2 2.2 copy-start.15
  509.1 2.3 copy-start.5
  514.7 2.2 copy-start.15
  522.5 37.2 %copy-start.17 = (bf16[4,1,1024,72]{2,3,1,0:T(8,128)(2,1)}, bf16[4,1,1024,72]{2,3,1,0:T(8,128)(2,1)S(1)}, u32[]{:S(2)}) copy-start(bf16[4,1,1024,72]{2,3,1,0:T(8,128)(2,1)S(1)} %get-tuple-element.92) | copy-start | bytes 1769476
  526.0 89.1 %reduce-scatter.18.cloned.1.call-start = ((), (), s32[]{:S(2)}) async-start(), calls=%async_computation.17 | async-start | bytes 2949120 | tf_op jit(solution)/shard_map/reduce_scatter | solution.py:201
  566.9 1.7 copy-start.32
  566.9 1.7 copy-start.34
  566.9 100.5 %all-gather.18.cloned.1.call-start = ((), (), s32[]{:S(2)}) async-start(), calls=%async_computation.13 | async-start | bytes 2949120 | tf_op jit(solution)/shard_map/all_gather | solution.py:216
  567.6 146.1 %reduce-scatter.20.cloned.1.call-start = ((), (), s32[]{:S(2)}) async-start(), calls=%async_computation.19 | async-start | bytes 2985984 | tf_op jit(solution)/shard_map/reduce_scatter | solution.py:230
  575.3 6.0 copy-start.12
  575.3 203.7 %reduce-scatter.22.cloned.1.call-start = ((), (), s32[]{:S(2)}) async-start(), calls=%async_computation.20 | async-start | bytes 6967296
  581.3 6.6 copy-start.19
  581.3 6.6 copy-start.40
  601.3 17.9 %copy-start.7 = (f32[1,256,1152]{2,1,0:T(8,128)S(1)}, f32[1,256,1152]{2,1,0:T(8,128)}, u32[]{:S(2)}) copy-start(f32[1,256,1152]{2,1,0:T(8,128)} %copy-done.6) | copy-start | bytes 3538948
  601.3 253.7 %all-gather.22.cloned.1.call-start = ((), (), s32[]{:S(2)}) async-start(), calls=%async_computation.18 | async-start | bytes 2949120 | tf_op jit(solution)/shard_map/all_gather | solution.py:217
  615.1 4.1 copy-start.10
  619.2 2.7 copy-start.28
  619.2 2.7 copy-start.27
  619.2 2.7 copy-start.26
  619.2 2.7 copy-start.25
  785.9 66.7 %copy-start.35 = (bf16[1,288]{1,0:T(2,128)(2,1)S(1)}, bf16[1,288]{1,0:T(2,128)(2,1)}, u32[]{:S(2)}) copy-start(bf16[1,288]{1,0:T(2,128)(2,1)} %param.13) | copy-start | bytes 1732
  785.9 66.7 %copy-start.36 = (f32[1,288]{1,0:T(1,128)S(1)}, f32[1,288]{1,0:T(1,128)}, u32[]{:S(2)}) copy-start(f32[1,288]{1,0:T(1,128)} %get-tuple-element.184) | copy-start | bytes 3460
  785.9 67.3 %copy-start.30 = (bf16[4,1,288]{2,1,0:T(2,128)(2,1)S(1)}, bf16[4,1,288]{2,1,0:T(2,128)(2,1)}, u32[]{:S(2)}) copy-start(bf16[4,1,288]{2,1,0:T(2,128)(2,1)} %copy-done.29) | copy-start | bytes 6916
  855.0 3.4 copy-start.14
  (19 other events, 24.5 us)
Sparse Core Ops, SparseCore 0:
  9.9 37.4 all-gather.9
  100.3 31.9 all-gather.11
  134.8 45.0 all-gather.13
  184.2 48.0 reduce-scatter.9
  236.8 49.9 all-gather.15
  311.1 46.8 reduce-scatter.13
  360.8 47.5 reduce-scatter.11
  414.6 49.9 all-gather.19
  526.1 33.5 reduce-scatter.15
  567.0 48.0 reduce-scatter.17
  617.3 49.9 all-gather.17
  671.1 42.5 reduce-scatter.19
  717.3 61.7 reduce-scatter.21
  781.1 55.2 all-gather.21

commit v2 on v1

--- a/solution.py
+++ b/solution.py
@@ -32,6 +32,37 @@
 def token_major(value_rows):
     head_count, latent_count, row_count, size = value_rows.shape
     return value_rows.transpose(1, 2, 0, 3).reshape(latent_count, row_count, head_count * size)
+
+
+def shifted(block, axis_name, step):
+    size = lax.axis_size(axis_name)
+    return lax.ppermute(block, axis_name, [(i, (i + step) % size) for i in range(size)])
+
+
+def gather_rows(block, axis_name):
+    size = lax.axis_size(axis_name)
+    position = lax.axis_index(axis_name)
+    rows = block.shape[1]
+    whole = jnp.zeros(block.shape[:1] + (size * rows,) + block.shape[2:], block.dtype)
+    whole = lax.dynamic_update_slice_in_dim(whole, block, position * rows, 1)
+    for step in range(1, size):
+        source = lax.rem(position - step + size, size)
+        whole = lax.dynamic_update_slice_in_dim(
+            whole, shifted(block, axis_name, step), source * rows, 1
+        )
+    return whole
+
+
+def scatter_sum(terms, axis_name):
+    size = lax.axis_size(axis_name)
+    position = lax.axis_index(axis_name)
+    rows = terms.shape[1] // size
+    total = lax.dynamic_slice_in_dim(terms, position * rows, rows, 1).astype(jnp.float32)
+    for step in range(1, size):
+        target = lax.rem(position + step, size)
+        part = lax.dynamic_slice_in_dim(terms, target * rows, rows, 1).astype(jnp.bfloat16)
+        total = total + shifted(part, axis_name, step).astype(jnp.float32)
+    return total
 
 
 def forward_head(operands):
@@ -104,12 +135,13 @@
     mod_terms = jnp.einsum(
         "bd,dkc->bkc", cond_all, modulation_weight, preferred_element_type=jnp.float32
     )
-    mod_parts = lax.all_gather(mod_terms, ("tp", "fsdp", "ctx"), axis=0)
-    mod_parts = lax.dynamic_slice_in_dim(mod_parts, own_latent, 1, 1)
-    column_parts = mod_parts.shape[0] // lax.axis_size("tp")
-    mod_parts = mod_parts.reshape((lax.axis_size("tp"), column_parts) + mod_parts.shape[2:])
-    modulations = jnp.sum(mod_parts, axis=0).transpose(1, 0, 2)
-    modulations = modulations.reshape(1, modulations.shape[0], -1)
+    vector_count, part_columns = mod_terms.shape[1:]
+    mod_terms = mod_terms.reshape(mod_terms.shape[0], -1)
+    mod_parts = jnp.sum(lax.all_gather(mod_terms, "tp", axis=0), axis=0)
+    mod_parts = lax.all_gather(lax.all_gather(mod_parts, "ctx", axis=0), "fsdp", axis=0)
+    mod_parts = lax.dynamic_slice_in_dim(mod_parts, own_latent, 1, 2)
+    mod_parts = mod_parts.reshape(-1, vector_count, part_columns)
+    modulations = mod_parts.transpose(1, 0, 2).reshape(1, vector_count, -1)
     shift_one = modulations[:, 0]
     scale_one = modulations[:, 1]
     gate_one = modulations[:, 2]
@@ -123,38 +155,26 @@
         "btd,dkc->btkc", act_one, qkv_full, preferred_element_type=jnp.float32
     ).astype(jnp.bfloat16)
     pair_local = projected[:, :, 1:]
-    pair_all = lax.all_gather(pair_local, "ctx", axis=1, tiled=True)
+    pair_all = gather_rows(pair_local, "ctx")
     heads_query = head_major(projected[:, :, 0])
     keys_heads = head_major(pair_all[:, :, 0])
     values_heads = head_major(pair_all[:, :, 1])
     mixed_values, logsum = lax.map(forward_head, (heads_query, keys_heads, values_heads))
     attended = token_major(mixed_values).astype(jnp.bfloat16)
-    branch_one = lax.psum_scatter(
-        jnp.einsum(
-            "btc,dc->btd", attended, out_t, preferred_element_type=jnp.float32
-        ).astype(jnp.bfloat16),
-        "tp",
-        scatter_dimension=1,
-        tiled=True,
-    ).astype(jnp.float32)
+    branch_one = scatter_sum(
+        jnp.einsum("btc,dc->btd", attended, out_t, preferred_element_type=jnp.float32), "tp"
+    )
     hidden = token_share + gate_one[:, None, :] * branch_one
     normed_two, norm_pull_two = jax.vjp(modulate, hidden, shift_two, scale_two)
-    act_two = lax.all_gather(normed_two.astype(jnp.bfloat16), "tp", axis=1, tiled=True)
+    act_two = gather_rows(normed_two.astype(jnp.bfloat16), "tp")
     pre_gelu = jnp.einsum("btd,df->btf", act_two, expand_full, preferred_element_type=jnp.float32)
     gelu_value, gelu_pull = jax.vjp(partial(jax.nn.gelu, approximate=True), pre_gelu)
     activated = gelu_value.astype(jnp.bfloat16)
-    branch_two = lax.psum_scatter(
-        jnp.einsum(
-            "btf,df->btd", activated, contract_t, preferred_element_type=jnp.float32
-        ).astype(jnp.bfloat16),
-        "tp",
-        scatter_dimension=1,
-        tiled=True,
-    ).astype(jnp.float32)
-    block_share = (hidden + gate_two[:, None, :] * branch_two).astype(jnp.bfloat16)
+    branch_two_terms = jnp.einsum(
+        "btf,df->btd", activated, contract_t, preferred_element_type=jnp.float32
+    ).astype(jnp.bfloat16)
     grad_out_full = cotangent.astype(jnp.float32)
     grad_out = lax.dynamic_slice_in_dim(grad_out_full, share_start, share_rows, 1)
-    grad_gate_two = jnp.sum(grad_out * branch_two, axis=1)
     grad_branch_two = (grad_out_full * gate_two[:, None, :]).astype(jnp.bfloat16)
     grad_activated = jnp.einsum(
         "btd,df->btf", grad_branch_two, contract_t, preferred_element_type=jnp.float32
@@ -163,59 +183,79 @@
     grad_contract = jnp.einsum(
         "btd,btf->df", grad_branch_two, activated, preferred_element_type=jnp.float32
     )
-    grad_act_two = lax.psum_scatter(
-        jnp.einsum(
-            "btf,df->btd", grad_pre, expand_full, preferred_element_type=jnp.float32
-        ).astype(jnp.bfloat16),
+    grad_act_two = scatter_sum(
+        jnp.einsum("btf,df->btd", grad_pre, expand_full, preferred_element_type=jnp.float32),
         "tp",
-        scatter_dimension=1,
-        tiled=True,
-    ).astype(jnp.float32)
+    )
     grad_expand = jnp.einsum("btd,btf->df", act_two, grad_pre, preferred_element_type=jnp.float32)
     grad_hidden, grad_shift_two, grad_scale_two = norm_pull_two(grad_act_two)
     grad_hidden = grad_hidden + grad_out
     grad_gate_one = jnp.sum(grad_hidden * branch_one, axis=1)
     branch_grad_share = (grad_hidden * gate_one[:, None, :]).astype(jnp.bfloat16)
-    grad_branch_one = lax.all_gather(branch_grad_share, "tp", axis=1, tiled=True)
+    grad_branch_one = gather_rows(branch_grad_share, "tp")
+    grad_branch_one, branch_two_terms, grad_expand, grad_contract = lax.optimization_barrier(
+        (
+            grad_branch_one,
+            branch_two_terms,
+            grad_expand.astype(jnp.bfloat16),
+            grad_contract.astype(jnp.bfloat16),
+        )
+    )
+    branch_two = scatter_sum(branch_two_terms, "tp")
     grad_attended = jnp.einsum(
         "btd,dc->btc", grad_branch_one, out_t, preferred_element_type=jnp.float32
     ).astype(jnp.bfloat16)
     grad_output = jnp.einsum(
         "btd,btc->dc", grad_branch_one, attended, preferred_element_type=jnp.float32
     )
-    grad_rest = jnp.concatenate((grad_output, grad_expand, grad_contract), axis=1)
-    grad_rest = lax.psum_scatter(
-        grad_rest.astype(jnp.bfloat16), everywhere, scatter_dimension=0, tiled=True
-    ).astype(jnp.float32)
+    grad_rest = jnp.concatenate(
+        (grad_output.astype(jnp.bfloat16), grad_expand, grad_contract), axis=1
+    )
+    grad_rest, grad_attended = lax.optimization_barrier((grad_rest, grad_attended))
+    grad_rest = lax.psum_scatter(grad_rest, everywhere, scatter_dimension=0, tiled=True)
     heads_grad = head_major(grad_attended)
-    grads_query, grads_keys, grads_values = lax.map(
-        backward_head, (heads_query, keys_heads, values_heads, heads_grad, logsum)
-    )
+    per_head = []
+    head_inputs = (heads_query, keys_heads, values_heads, heads_grad, logsum)
+    head_count = heads_query.shape[0]
+    for head in range(head_count):
+        operands = tuple(array[head] for array in head_inputs)
+        if head == max(head_count // 2, 1):
+            operands, per_head[-1], branch_two = lax.optimization_barrier(
+                (operands, per_head[-1], branch_two)
+            )
+        elif head > 0:
+            operands, per_head[-1] = lax.optimization_barrier((operands, per_head[-1]))
+        per_head.append(backward_head(operands))
+    block_share = (hidden + gate_two[:, None, :] * branch_two).astype(jnp.bfloat16)
+    grad_gate_two = jnp.sum(grad_out * branch_two, axis=1)
+    block_out = gather_rows(block_share, "tp")
+    per_head[-1], block_out, grad_rest = lax.optimization_barrier(
+        (per_head[-1], block_out, grad_rest)
+    )
+    grads_query, grads_keys, grads_values = (jnp.stack(parts) for parts in zip(*per_head))
     pair_terms = jnp.stack((token_major(grads_keys), token_major(grads_values)), axis=2)
-    pair_terms = pair_terms.astype(jnp.bfloat16)
-    grad_pair = lax.psum_scatter(pair_terms, "ctx", scatter_dimension=1, tiled=True).astype(
-        jnp.bfloat16
-    )
+    grad_pair = scatter_sum(pair_terms, "ctx").astype(jnp.bfloat16)
     grad_query = token_major(grads_query).astype(jnp.bfloat16)
     grad_projected = jnp.concatenate((grad_query[:, :, None], grad_pair), axis=2)
-    grad_act_one = lax.psum_scatter(
+    grad_act_one = scatter_sum(
         jnp.einsum(
             "btkc,dkc->btd", grad_projected, qkv_full, preferred_element_type=jnp.float32
-        ).astype(jnp.bfloat16),
+        ),
         "tp",
-        scatter_dimension=1,
-        tiled=True,
-    ).astype(jnp.float32)
+    )
+    grad_rest = grad_rest.astype(jnp.float32)
     grad_attention = jnp.einsum(
         "btd,btkc->dkc", act_one, grad_projected, preferred_element_type=jnp.float32
     )
+    grad_attention = lax.psum_scatter(
+        grad_attention.astype(jnp.bfloat16), everywhere, scatter_dimension=0, tiled=True
+    )
+    grad_act_one, grad_attention = lax.optimization_barrier((grad_act_one, grad_attention))
+    grad_attention = grad_attention.astype(jnp.float32)
     normed_share, norm_pull_one = jax.vjp(modulate, token_share, shift_one, scale_one)
     grad_tokens, grad_shift_one, grad_scale_one = norm_pull_one(grad_act_one)
     grad_tokens = grad_tokens + grad_hidden
-    block_out, latents_grad = (
-        lax.all_gather(block_share, "tp", axis=1, tiled=True),
-        lax.all_gather(grad_tokens.astype(jnp.bfloat16), "tp", axis=1, tiled=True),
-    )
+    latents_grad = gather_rows(grad_tokens.astype(jnp.bfloat16), "tp")
     grad_parts = jnp.stack(
         (
             grad_shift_one,
@@ -227,14 +267,11 @@
         ),
         axis=1,
     )
-    grad_attention = lax.psum_scatter(
-        grad_attention.astype(jnp.bfloat16), everywhere, scatter_dimension=0, tiled=True
-    ).astype(jnp.float32)
-    grad_modulations = lax.all_gather(grad_parts[0], ("ctx", "tp", "fsdp"), axis=0)
-    latent_count = lax.axis_size("fsdp")
-    grad_modulations = jnp.sum(
-        grad_modulations.reshape((-1, latent_count) + grad_modulations.shape[1:]), axis=0
-    )
+    grad_parts = grad_parts.reshape(1, -1)
+    grad_sums = jnp.sum(lax.all_gather(grad_parts, "tp", axis=0), axis=0)
+    grad_sums = jnp.sum(lax.all_gather(grad_sums, "ctx", axis=0), axis=0)
+    grad_modulations = lax.all_gather(grad_sums, "fsdp", axis=0, tiled=True)
+    grad_modulations = grad_modulations.reshape(grad_modulations.shape[0], vector_count, -1)
     column_count = modulation_weight.shape[2]
     column_start = lax.axis_index(everywhere) * column_count
     grad_columns = lax.dynamic_slice_in_dim(grad_modulations, column_start, column_count, 2)

time: 876 us -> 728 us (0.83)
  waiting for transfers between devices: 462 us -> 243 us
  starting transfers between devices: 2 us -> 121 us
  blocking collectives: 146 us -> 111 us
  matrix products: 141 us -> 127 us
    ppermute x0 -> x26, waiting for transfers between devices: none -> 242 us  [shifted(): lax.ppermute(block, axis_name, [(i, (i + step) % size) for i in range(siz...]
    all_gather x5 -> x0, waiting for transfers between devices: 174 us -> none  [the longest x1 50.1 us: shards(): lax.all_gather(normed_two.astype(jnp.bfloat16), 'tp', axis=1, tiled=True)]
    reduce_scatter x5 -> x1, waiting for transfers between devices: 170 us -> 0.01 us  [shards(): lax.psum_scatter(grad_rest, everywhere, scatter_dimension=0, tiled=True)]
    ppermute x0 -> x26, starting transfers between devices: none -> 121 us  [shifted(): lax.ppermute(block, axis_name, [(i, (i + step) % size) for i in range(siz...]
    unnamed x15 -> x4, waiting for transfers between devices: 65.1 us -> 0.73 us
    reduce_scatter x1, waiting for transfers between devices: 46.3 us -> 0.02 us  [shards(): lax.psum_scatter(grad_attention.astype(jnp.bfloat16), everywhere, scatter...]
    all_gather x2 -> x6, blocking collectives: 127 us -> 90.7 us  [the longest x1 56.4 us: shards(): grad_sums = jnp.sum(lax.all_gather(grad_parts, 'tp', axis=0), axis=0)]
    unnamed x88 -> x143, local copies, waits for them, and re-layouts: 27.5 us -> 7.14 us
  transfers between devices with their start and end apart: 14 -> 30, of which waited for: 12 -> 17; matrix products, arithmetic and copies ran while one was open for 14% -> 18% of each run, Pallas kernels for 0% -> 0%
where the time goes in v2:
time: 728 us; the launch traced here: 722 us
  waiting for transfers between devices  243 us (33%)
  matrix products  127 us (17%)
  starting transfers between devices  121 us (17%)
  blocking collectives  111 us (15%)
  other arithmetic  52.8 us (7%)
  local copies, waits for them, and re-layouts  51.9 us (7%)
  between operations  15.1 us (2%)
    ppermute x26, waiting for transfers between devices, shifted(): lax.ppermute(block, axis_name, [(i, (i + step) % size) for i in range(siz...  242 us
    ppermute x26, starting transfers between devices, shifted(): lax.ppermute(block, axis_name, [(i, (i + step) % size) for i in range(siz...  121 us
    all_gather x1, blocking collectives, shards(): grad_sums = jnp.sum(lax.all_gather(grad_parts, 'tp', axis=0), axis=0)  56.4 us
    dot_general x4, matrix products, backward_head(): jnp.einsum('vft,vfm->vtm', probabilities.astype(jnp.bfloat16), grad_mixed...  16.6 us
  transfers between devices with their start and end apart: 30, of which 17 were waited for; matrix products, arithmetic and copies ran while one was open for 18% of the time, Pallas kernels for 0%

profile of v2, /device:TPU:0, one launch (start us, length us, event | category | flops | bytes accessed | tf_op | source)
XLA Modules:
  0.0 722.3 jit_solution(16615526798224298670)
XLA Ops:
  9.3 6.1 all-gather.4
  16.1 13.9 %all_gather.37 = f32[4,4,864]{2,1,0:T(4,128)S(1)} all-gather(f32[1,4,864]{2,1,0:T(4,128)S(1)} %all_gather_reshape.6), channel_id=1, replica_groups=mesh['fsdp'=4,'ctx'=2,'tp'=4] {'tp'}, dimensions={0}, use_global_device_ids=true | all-gather | bytes 69120 | tf_op jit(solution)/shard_map/all_gather | solution.py:140
  30.1 4.4 all-gather.5
  34.5 6.0 all-gather.1
  44.9 4.6 convert_bitcast_fusion
  61.8 4.3 convert_element_type.251
  66.8 23.1 %collective-permute-done = bf16[1,1024,2,288]{1,3,2,0:T(8,128)(2,1)} collective-permute-done((bf16[1,1024,2,288]{1,3,2,0:T(8,128)(2,1)}, bf16[1,1024,2,288]{1,3,2,0:T(8,128)(2,1)}, u32[]{:S(2)}, u32[]{:S(2)}) %collective-permute-start) | collective-permute-done | bytes 1179680 | tf_op jit(solution)/shard_map/ppermute | solution.py:39
  95.4 29.3 %while.12 = (s32[]{:T(128)}, bf16[4,1,1024,72]{2,3,1,0:T(8,128)(2,1)S(1)}, f32[4,1,1024]{2,1,0:T(1,128)}, bf16[4,1,1024,72]{3,2,1,0:T(8,128)(2,1)S(1)}, bf16[4,1...) while((s32[]{:T(128)}, bf16[4,1,1024,72]{2,3,1,0:T(8,128)(2,1)S(1)}, ...), condition=%wide.region_6.7_spmd, body=%wide.region_3.6_spmd.sunk | while | flops 622853120 | bytes 26356300 | solution.py:162
  99.3 3.4 fusion.180
  106.6 3.4 fusion.180
  113.9 3.4 fusion.180
  121.3 3.4 fusion.180
  134.3 12.2 %collective-permute-done.1 = bf16[1,256,1152]{2,1,0:T(8,128)(2,1)S(1)} collective-permute-done((bf16[1,256,1152]{2,1,0:T(8,128)(2,1)S(1)}, bf16[1,256,1152]{2,1,0:T(8,128)(2,1)S(1)}, u32[]{:S(2)}, u32[]{:S(2)}) %collective-permute-start.1) | collective-permute-done | bytes 589856 | tf_op jit(solution)/shard_map/ppermute | solution.py:39
  146.5 23.8 %collective-permute-done.2 = bf16[1,256,1152]{2,1,0:T(8,128)(2,1)S(1)} collective-permute-done((bf16[1,256,1152]{2,1,0:T(8,128)(2,1)S(1)}, bf16[1,256,1152]{2,1,0:T(8,128)(2,1)S(1)}, u32[]{:S(2)}, u32[]{:S(2)}) %collective-permute-start.2) | collective-permute-done | bytes 589856 | tf_op jit(solution)/shard_map/ppermute | solution.py:39
  173.8 13.1 %collective-permute-start.4 = (bf16[1,256,1152]{2,1,0:T(8,128)(2,1)S(1)}, bf16[1,256,1152]{2,1,0:T(8,128)(2,1)S(1)}, u32[]{:S(2)}, u32[]{:S(2)}) collective-permute-start(bf16[1,256,1152]{2,1,0:T(8,128)(2,1)S(1)} %get-tuple-element.181), channel_id=1, source_target_pairs={{0,1},{1,2},{2,3},{3,0},{4,5},{5,6},{6,7},{7,4},{8,9},{9,10},{10,1... | collective-permute-start | bytes 1769480 | tf_op jit(solution)/shard_map/ppermute | solution.py:39
  187.0 5.5 fusion.121
  196.1 4.9 collective-permute-done.4
  201.0 23.2 %collective-permute-done.5 = bf16[1,256,1152]{2,1,0:T(8,128)(2,1)S(1)} collective-permute-done((bf16[1,256,1152]{2,1,0:T(8,128)(2,1)S(1)}, bf16[1,256,1152]{2,1,0:T(8,128)(2,1)S(1)}, u32[]{:S(2)}, u32[]{:S(2)}) %collective-permute-start.5) | collective-permute-done | bytes 589856 | tf_op jit(solution)/shard_map/ppermute | solution.py:39
  225.2 3.6 fusion.62
  228.8 4.9 convolution_convert_fusion
  233.7 8.1 %fusion.24 = bf16[1024,1152]{1,0:T(8,128)(2,1)} fusion(f32[1024,1152]{1,0:T(8,128)S(1)} %fusion.62, bf16[1152,2592]{1,0:T(8,128)(2,1)S(1)} %bitcast.371, f32[1152]{0:T(1024)S(1)} %copy-done.44, bf16[1,1024,1152]{2,1,0:T(8,128)(2,1)S(1)} %copy-done.18), kind=kOutput, calls=%fused_computation.49 | convolution fusion | flops 2745040896 | bytes 12099584 | tf_op jit(solution)/shard_map/btd,df->btf/dot_general | solution.py:179
  241.8 5.3 fusion.60
  247.3 13.0 %collective-permute-start.7 = (bf16[1,256,1152]{2,1,0:T(8,128)(2,1)S(1)}, bf16[1,256,1152]{2,1,0:T(8,128)(2,1)S(1)}, u32[]{:S(2)}, u32[]{:S(2)}) collective-permute-start(bf16[1,256,1152]{2,1,0:T(8,128)(2,1)S(1)} %get-tuple-element.192), channel_id=1, source_target_pairs={{0,1},{1,2},{2,3},{3,0},{4,5},{5,6},{6,7},{7,4},{8,9},{9,10},{10,1... | collective-permute-start | bytes 1769480 | tf_op jit(solution)/shard_map/ppermute | solution.py:39
  263.7 6.0 fusion.33
  269.7 7.8 %collective-permute-done.7 = bf16[1,256,1152]{2,1,0:T(8,128)(2,1)S(1)} collective-permute-done((bf16[1,256,1152]{2,1,0:T(8,128)(2,1)S(1)}, bf16[1,256,1152]{2,1,0:T(8,128)(2,1)S(1)}, u32[]{:S(2)}, u32[]{:S(2)}) %collective-permute-start.7) | collective-permute-done | bytes 589856 | tf_op jit(solution)/shard_map/ppermute | solution.py:39
  277.5 24.0 %collective-permute-done.8 = bf16[1,256,1152]{2,1,0:T(8,128)(2,1)S(1)} collective-permute-done((bf16[1,256,1152]{2,1,0:T(8,128)(2,1)S(1)}, bf16[1,256,1152]{2,1,0:T(8,128)(2,1)S(1)}, u32[]{:S(2)}, u32[]{:S(2)}) %collective-permute-start.8) | collective-permute-done | bytes 589856 | tf_op jit(solution)/shard_map/ppermute | solution.py:39
  305.8 13.2 %collective-permute-start.10 = (bf16[1,256,1152]{2,1,0:T(8,128)(2,1)S(1)}, bf16[1,256,1152]{2,1,0:T(8,128)(2,1)S(1)}, u32[]{:S(2)}, u32[]{:S(2)}) collective-permute-start(bf16[1,256,1152]{2,1,0:T(8,128)(2,1)S(1)} %get-tuple-element.176), channel_id=1, source_target_pairs={{0,1},{1,2},{2,3},{3,0},{4,5},{5,6},{6,7},{7,4},{8,9},{9,10},{10,1... | collective-permute-start | bytes 1769480 | tf_op jit(solution)/shard_map/ppermute | solution.py:39
  321.6 4.8 convolution_convert_fusion.1
  326.5 6.2 collective-permute-done.10
  332.8 23.0 %collective-permute-done.11 = bf16[1,256,1152]{2,1,0:T(8,128)(2,1)S(1)} collective-permute-done((bf16[1,256,1152]{2,1,0:T(8,128)(2,1)S(1)}, bf16[1,256,1152]{2,1,0:T(8,128)(2,1)S(1)}, u32[]{:S(2)}, u32[]{:S(2)}) %collective-permute-start.11) | collective-permute-done | bytes 589856 | tf_op jit(solution)/shard_map/ppermute | solution.py:39
  362.7 11.3 %concatenate.10 = bf16[1152,2592]{1,0:T(8,128)(2,1)} concatenate(bf16[1152,288]{1,0:T(8,128)(2,1)} %copy.51, bf16[1152,1152]{1,0:T(8,128)(2,1)} %convolution_convert_fusion.1, bf16[1152,1152]{1,0:T(8,128)(2,1)} %convolution_convert_fusion), dimensions={1} | concatenate | bytes 11943936 | tf_op jit(solution)/shard_map/concatenate | solution.py:211
  377.0 5.9 fusion.44
  395.0 13.4 %collective-permute-start.13 = (bf16[1,256,1152]{2,1,0:T(8,128)(2,1)}, bf16[1,256,1152]{2,1,0:T(8,128)(2,1)}, u32[]{:S(2)}, u32[]{:S(2)}) collective-permute-start(bf16[1,256,1152]{2,1,0:T(8,128)(2,1)} %get-tuple-element.198), channel_id=1, source_target_pairs={{0,1},{1,2},{2,3},{3,0},{4,5},{5,6},{6,7},{7,4},{8,9},{9,10},{10,1... | collective-permute-start | bytes 1769480 | tf_op jit(solution)/shard_map/ppermute | solution.py:39
  422.3 5.8 fusion.47
  428.1 21.8 %collective-permute-done.14 = bf16[1,256,1152]{2,1,0:T(8,128)(2,1)} collective-permute-done((bf16[1,256,1152]{2,1,0:T(8,128)(2,1)}, bf16[1,256,1152]{2,1,0:T(8,128)(2,1)}, u32[]{:S(2)}, u32[]{:S(2)}) %collective-permute-start.14) | collective-permute-done | bytes 589856 | tf_op jit(solution)/shard_map/ppermute | solution.py:39
  454.3 13.1 %collective-permute-start.16 = (bf16[1,256,1152]{2,1,0:T(8,128)(2,1)S(1)}, bf16[1,256,1152]{2,1,0:T(8,128)(2,1)S(1)}, u32[]{:S(2)}, u32[]{:S(2)}) collective-permute-start(bf16[1,256,1152]{2,1,0:T(8,128)(2,1)S(1)} %get-tuple-element.174), channel_id=1, source_target_pairs={{0,1},{1,2},{2,3},{3,0},{4,5},{5,6},{6,7},{7,4},{8,9},{9,10},{10,1... | collective-permute-start | bytes 1769480 | tf_op jit(solution)/shard_map/ppermute | solution.py:39
  494.2 9.9 %collective-permute-done.17 = bf16[1,256,1152]{2,1,0:T(8,128)(2,1)S(1)} collective-permute-done((bf16[1,256,1152]{2,1,0:T(8,128)(2,1)S(1)}, bf16[1,256,1152]{2,1,0:T(8,128)(2,1)S(1)}, u32[]{:S(2)}, u32[]{:S(2)}) %collective-permute-start.17) | collective-permute-done | bytes 589856 | tf_op jit(solution)/shard_map/ppermute | solution.py:39
  510.6 25.7 %collective-permute-done.19 = bf16[1,1024,2,288]{1,3,2,0:T(8,128)(2,1)S(1)} collective-permute-done((bf16[1,1024,2,288]{1,3,2,0:T(8,128)(2,1)S(1)}, bf16[1,1024,2,288]{1,3,2,0:T(8,128)(2,1)S(1)}, u32[]{:S(2)}, u32[]{:S(2)}) %collective-permute-start.19) | collective-permute-done | bytes 1179680 | tf_op jit(solution)/shard_map/ppermute | solution.py:39
  537.8 5.3 convolution_convert_fusion.2
  545.8 3.7 convolution_bitcast_fusion
  549.7 13.9 %collective-permute-start.20 = (bf16[1,256,1152]{2,1,0:T(8,128)(2,1)S(1)}, bf16[1,256,1152]{2,1,0:T(8,128)(2,1)S(1)}, u32[]{:S(2)}, u32[]{:S(2)}) collective-permute-start(bf16[1,256,1152]{2,1,0:T(8,128)(2,1)S(1)} %get-tuple-element.189), channel_id=1, source_target_pairs={{0,1},{1,2},{2,3},{3,0},{4,5},{5,6},{6,7},{7,4},{8,9},{9,10},{10,1... | collective-permute-start | bytes 1769480 | tf_op jit(solution)/shard_map/ppermute | solution.py:39
  570.0 10.8 %collective-permute-done.20 = bf16[1,256,1152]{2,1,0:T(8,128)(2,1)S(1)} collective-permute-done((bf16[1,256,1152]{2,1,0:T(8,128)(2,1)S(1)}, bf16[1,256,1152]{2,1,0:T(8,128)(2,1)S(1)}, u32[]{:S(2)}, u32[]{:S(2)}) %collective-permute-start.20) | collective-permute-done | bytes 589856 | tf_op jit(solution)/shard_map/ppermute | solution.py:39
  580.8 23.1 %collective-permute-done.21 = bf16[1,256,1152]{2,1,0:T(8,128)(2,1)S(1)} collective-permute-done((bf16[1,256,1152]{2,1,0:T(8,128)(2,1)S(1)}, bf16[1,256,1152]{2,1,0:T(8,128)(2,1)S(1)}, u32[]{:S(2)}, u32[]{:S(2)}) %collective-permute-start.21) | collective-permute-done | bytes 589856 | tf_op jit(solution)/shard_map/ppermute | solution.py:39
  609.0 13.1 %collective-permute-start.23 = (bf16[1,256,1152]{2,1,0:T(8,128)(2,1)}, bf16[1,256,1152]{2,1,0:T(8,128)(2,1)}, u32[]{:S(2)}, u32[]{:S(2)}) collective-permute-start(bf16[1,256,1152]{2,1,0:T(8,128)(2,1)} %get-tuple-element.170), channel_id=1, source_target_pairs={{0,1},{1,2},{2,3},{3,0},{4,5},{5,6},{6,7},{7,4},{8,9},{9,10},{10,1... | collective-permute-start | bytes 1769480 | tf_op jit(solution)/shard_map/ppermute | solution.py:39
  624.6 56.4 %all_gather.44 = f32[4,1,6912]{2,1,0:T(1,128)S(1)} all-gather(f32[1,1,6912]{2,1,0:T(1,128)S(1)} %all_gather_reshape.7), channel_id=1, replica_groups=mesh['fsdp'=4,'ctx'=2,'tp'=4] {'tp'}, dimensions={0}, use_global_device_ids=true | all-gather | bytes 138240 | tf_op jit(solution)/shard_map/all_gather | solution.py:271
  681.2 4.5 all-gather.6
  685.8 5.4 all-gather.7
  693.9 14.3 %psum.7 = f32[4,288]{1,0:T(4,128)S(1)} all-reduce(f32[4,288]{1,0:T(4,128)S(1)} %convolution_bitcast_fusion.1), channel_id=1, replica_groups=mesh['fsdp'=4,'ctx'=2,'tp'=4] {'fsdp','ctx'}, use_global_device_ids=true, to_apply=%region_29.30 | all-reduce | flops 1152 | bytes 9216 | tf_op jit(solution)/shard_map/psum | solution.py:285
  (327 shorter events, 170.6 us)
Async XLA Ops:
  7.2 36.4 %copy-start.2 = (bf16[1,1024,1152]{2,1,0:T(8,128)(2,1)S(1)}, bf16[1,1024,1152]{2,1,0:T(8,128)(2,1)}, u32[]{:S(2)}) copy-start(bf16[1,1024,1152]{2,1,0:T(8,128)(2,1)} %param.10) | copy-start | bytes 7077892
  7.2 37.2 %all-gather.11.cloned.1.call-start = ((), (), s32[]{:S(2)}) async-start(), calls=%async_computation.2 | async-start | bytes 2985984 | tf_op jit(solution)/shard_map/all_gather | solution.py:120
  7.9 116.8 %all-gather.13.cloned.1.call-start = ((), (), s32[]{:S(2)}) async-start(), calls=%async_computation.3 | async-start | bytes 6967296 | tf_op jit(solution)/shard_map/all_gather | solution.py:123
  53.1 36.8 %collective-permute-start = (bf16[1,1024,2,288]{1,3,2,0:T(8,128)(2,1)}, bf16[1,1024,2,288]{1,3,2,0:T(8,128)(2,1)}, u32[]{:S(2)}, u32[]{:S(2)}) collective-permute-start(bf16[1,1024,2,288]{1,3,2,0:T(8,128)(2,1)} %get-tuple-element.203), channel_id=1, source_target_pairs={{0,4},{4,0},{1,5},{5,1},{2,6},{6,2},{3,7},{7,3},{8,12},{12,8},{9,1... | collective-permute-start | bytes 3538952 | tf_op jit(solution)/shard_map/ppermute | solution.py:39
  57.0 449.4 %reduce-scatter.3.cloned.1.call-start = ((), (), s32[]{:S(2)}) async-start(), calls=%async_computation.4 | async-start | bytes 6967296 | tf_op jit(solution)/shard_map/reduce_scatter | solution.py:215
  128.2 42.1 %copy-start.43 = (f32[1152]{0:T(1024)S(1)}, f32[1152]{0:T(1024)}, u32[]{:S(2)}) copy-start(f32[1152]{0:T(1024)} %get-tuple-element.152) | copy-start | bytes 13828
  128.3 42.1 %copy-start.55 = (f32[256]{0:T(256)S(1)}, f32[256]{0:T(256)}, u32[]{:S(2)}) copy-start(f32[256]{0:T(256)} %broadcast_multiply_fusion.1) | copy-start | bytes 3076
  128.3 18.2 %collective-permute-start.1 = (bf16[1,256,1152]{2,1,0:T(8,128)(2,1)S(1)}, bf16[1,256,1152]{2,1,0:T(8,128)(2,1)S(1)}, u32[]{:S(2)}, u32[]{:S(2)}) collective-permute-start(bf16[1,256,1152]{2,1,0:T(8,128)(2,1)S(1)} %get-tuple-element.195), channel_id=1, source_target_pairs={{0,1},{1,2},{2,3},{3,0},{4,5},{5,6},{6,7},{7,4},{8,9},{9,10},{10,1... | collective-permute-start | bytes 1769480 | tf_op jit(solution)/shard_map/ppermute | solution.py:39
  129.9 40.5 %collective-permute-start.2 = (bf16[1,256,1152]{2,1,0:T(8,128)(2,1)S(1)}, bf16[1,256,1152]{2,1,0:T(8,128)(2,1)S(1)}, u32[]{:S(2)}, u32[]{:S(2)}) collective-permute-start(bf16[1,256,1152]{2,1,0:T(8,128)(2,1)S(1)} %get-tuple-element.197), channel_id=1, source_target_pairs={{0,2},{1,3},{2,0},{3,1},{4,6},{5,7},{6,4},{7,5},{8,10},{9,11},{10,... | collective-permute-start | bytes 1769480 | tf_op jit(solution)/shard_map/ppermute | solution.py:39
  132.3 38.1 %collective-permute-start.3 = (bf16[1,256,1152]{2,1,0:T(8,128)(2,1)S(1)}, bf16[1,256,1152]{2,1,0:T(8,128)(2,1)S(1)}, u32[]{:S(2)}, u32[]{:S(2)}) collective-permute-start(bf16[1,256,1152]{2,1,0:T(8,128)(2,1)S(1)} %get-tuple-element.196), channel_id=1, source_target_pairs={{0,3},{1,0},{2,1},{3,2},{4,7},{5,4},{6,5},{7,6},{8,11},{9,8},{10,9... | collective-permute-start | bytes 1769480 | tf_op jit(solution)/shard_map/ppermute | solution.py:39
  173.8 51.3 %slice-start.3 = ((s8[6193152]{0:T(1024)(128)(4,1)}), s8[4194304]{0:T(1024)(128)(4,1)S(1)}, s32[]{:S(2)}) async-start(s8[6193152]{0:T(1024)(128)(4,1)} %bitcast.370), calls=%async_computation.9 | async-start | bytes 8388608
  173.8 19.4 %copy-start.54 = (f32[4,1,1024]{2,1,0:T(1,128)S(1)}, f32[4,1,1024]{2,1,0:T(1,128)}, u32[]{:S(2)}) copy-start(f32[4,1,1024]{2,1,0:T(1,128)} %get-tuple-element.84) | copy-start | bytes 49156
  173.8 51.3 %slice-start.4 = ((s8[6193152]{0:T(1024)(128)(4,1)}), s8[1998848]{0:T(1024)(128)(4,1)S(1)}, s32[]{:S(2)}) async-start(s8[6193152]{0:T(1024)(128)(4,1)} %bitcast.370), calls=%async_computation.10 | async-start | bytes 3997696
  173.8 27.1 %collective-permute-start.4 = (bf16[1,256,1152]{2,1,0:T(8,128)(2,1)S(1)}, bf16[1,256,1152]{2,1,0:T(8,128)(2,1)S(1)}, u32[]{:S(2)}, u32[]{:S(2)}) collective-permute-start(bf16[1,256,1152]{2,1,0:T(8,128)(2,1)S(1)} %get-tuple-element.181), channel_id=1, source_target_pairs={{0,1},{1,2},{2,3},{3,0},{4,5},{5,6},{6,7},{7,4},{8,9},{9,10},{10,1... | collective-permute-start | bytes 1769480 | tf_op jit(solution)/shard_map/ppermute | solution.py:39
  192.4 31.8 %collective-permute-start.5 = (bf16[1,256,1152]{2,1,0:T(8,128)(2,1)S(1)}, bf16[1,256,1152]{2,1,0:T(8,128)(2,1)S(1)}, u32[]{:S(2)}, u32[]{:S(2)}) collective-permute-start(bf16[1,256,1152]{2,1,0:T(8,128)(2,1)S(1)} %get-tuple-element.181), channel_id=1, source_target_pairs={{0,2},{1,3},{2,0},{3,1},{4,6},{5,7},{6,4},{7,5},{8,10},{9,11},{10,... | collective-permute-start | bytes 1769480 | tf_op jit(solution)/shard_map/ppermute | solution.py:39
  193.8 31.3 %collective-permute-start.6 = (bf16[1,256,1152]{2,1,0:T(8,128)(2,1)S(1)}, bf16[1,256,1152]{2,1,0:T(8,128)(2,1)S(1)}, u32[]{:S(2)}, u32[]{:S(2)}) collective-permute-start(bf16[1,256,1152]{2,1,0:T(8,128)(2,1)S(1)} %get-tuple-element.181), channel_id=1, source_target_pairs={{0,3},{1,0},{2,1},{3,2},{4,7},{5,4},{6,5},{7,6},{8,11},{9,8},{10,9... | collective-permute-start | bytes 1769480 | tf_op jit(solution)/shard_map/ppermute | solution.py:39
  247.3 30.2 %collective-permute-start.7 = (bf16[1,256,1152]{2,1,0:T(8,128)(2,1)S(1)}, bf16[1,256,1152]{2,1,0:T(8,128)(2,1)S(1)}, u32[]{:S(2)}, u32[]{:S(2)}) collective-permute-start(bf16[1,256,1152]{2,1,0:T(8,128)(2,1)S(1)} %get-tuple-element.192), channel_id=1, source_target_pairs={{0,1},{1,2},{2,3},{3,0},{4,5},{5,6},{6,7},{7,4},{8,9},{9,10},{10,1... | collective-permute-start | bytes 1769480 | tf_op jit(solution)/shard_map/ppermute | solution.py:39
  260.3 41.2 %collective-permute-start.8 = (bf16[1,256,1152]{2,1,0:T(8,128)(2,1)S(1)}, bf16[1,256,1152]{2,1,0:T(8,128)(2,1)S(1)}, u32[]{:S(2)}, u32[]{:S(2)}) collective-permute-start(bf16[1,256,1152]{2,1,0:T(8,128)(2,1)S(1)} %get-tuple-element.194), channel_id=1, source_target_pairs={{0,2},{1,3},{2,0},{3,1},{4,6},{5,7},{6,4},{7,5},{8,10},{9,11},{10,... | collective-permute-start | bytes 1769480 | tf_op jit(solution)/shard_map/ppermute | solution.py:39
  263.7 37.8 %collective-permute-start.9 = (bf16[1,256,1152]{2,1,0:T(8,128)(2,1)S(1)}, bf16[1,256,1152]{2,1,0:T(8,128)(2,1)S(1)}, u32[]{:S(2)}, u32[]{:S(2)}) collective-permute-start(bf16[1,256,1152]{2,1,0:T(8,128)(2,1)S(1)} %get-tuple-element.193), channel_id=1, source_target_pairs={{0,3},{1,0},{2,1},{3,2},{4,7},{5,4},{6,5},{7,6},{8,11},{9,8},{10,9... | collective-permute-start | bytes 1769480 | tf_op jit(solution)/shard_map/ppermute | solution.py:39
  305.5 21.0 %copy-start.5 = (f32[1,256,1152]{2,1,0:T(8,128)}, f32[1,256,1152]{2,1,0:T(8,128)S(1)}, u32[]{:S(2)}) copy-start(f32[1,256,1152]{2,1,0:T(8,128)S(1)} %get-tuple-element.168) | copy-start | bytes 3538948
  305.8 26.9 %collective-permute-start.10 = (bf16[1,256,1152]{2,1,0:T(8,128)(2,1)S(1)}, bf16[1,256,1152]{2,1,0:T(8,128)(2,1)S(1)}, u32[]{:S(2)}, u32[]{:S(2)}) collective-permute-start(bf16[1,256,1152]{2,1,0:T(8,128)(2,1)S(1)} %get-tuple-element.176), channel_id=1, source_target_pairs={{0,1},{1,2},{2,3},{3,0},{4,5},{5,6},{6,7},{7,4},{8,9},{9,10},{10,1... | collective-permute-start | bytes 1769480 | tf_op jit(solution)/shard_map/ppermute | solution.py:39
  319.0 36.7 %collective-permute-start.11 = (bf16[1,256,1152]{2,1,0:T(8,128)(2,1)S(1)}, bf16[1,256,1152]{2,1,0:T(8,128)(2,1)S(1)}, u32[]{:S(2)}, u32[]{:S(2)}) collective-permute-start(bf16[1,256,1152]{2,1,0:T(8,128)(2,1)S(1)} %get-tuple-element.176), channel_id=1, source_target_pairs={{0,2},{1,3},{2,0},{3,1},{4,6},{5,7},{6,4},{7,5},{8,10},{9,11},{10,... | collective-permute-start | bytes 1769480 | tf_op jit(solution)/shard_map/ppermute | solution.py:39
  319.0 38.1 %collective-permute-start.12 = (bf16[1,256,1152]{2,1,0:T(8,128)(2,1)S(1)}, bf16[1,256,1152]{2,1,0:T(8,128)(2,1)S(1)}, u32[]{:S(2)}, u32[]{:S(2)}) collective-permute-start(bf16[1,256,1152]{2,1,0:T(8,128)(2,1)S(1)} %get-tuple-element.176), channel_id=1, source_target_pairs={{0,3},{1,0},{2,1},{3,2},{4,7},{5,4},{6,5},{7,6},{8,11},{9,8},{10,9... | collective-permute-start | bytes 1769480 | tf_op jit(solution)/shard_map/ppermute | solution.py:39
  326.5 32.1 %copy-start.24 = (bf16[4,1,1024,72]{2,3,1,0:T(8,128)(2,1)S(1)}, bf16[4,1,1024,72]{2,3,1,0:T(8,128)(2,1)}, u32[]{:S(2)}) copy-start(bf16[4,1,1024,72]{2,3,1,0:T(8,128)(2,1)} %copy-done.23) | copy-start | bytes 1769476
  395.0 33.1 %collective-permute-start.13 = (bf16[1,256,1152]{2,1,0:T(8,128)(2,1)}, bf16[1,256,1152]{2,1,0:T(8,128)(2,1)}, u32[]{:S(2)}, u32[]{:S(2)}) collective-permute-start(bf16[1,256,1152]{2,1,0:T(8,128)(2,1)} %get-tuple-element.198), channel_id=1, source_target_pairs={{0,1},{1,2},{2,3},{3,0},{4,5},{5,6},{6,7},{7,4},{8,9},{9,10},{10,1... | collective-permute-start | bytes 1769480 | tf_op jit(solution)/shard_map/ppermute | solution.py:39
  408.3 41.6 %collective-permute-start.14 = (bf16[1,256,1152]{2,1,0:T(8,128)(2,1)}, bf16[1,256,1152]{2,1,0:T(8,128)(2,1)}, u32[]{:S(2)}, u32[]{:S(2)}) collective-permute-start(bf16[1,256,1152]{2,1,0:T(8,128)(2,1)} %get-tuple-element.200), channel_id=1, source_target_pairs={{0,2},{1,3},{2,0},{3,1},{4,6},{5,7},{6,4},{7,5},{8,10},{9,11},{10,... | collective-permute-start | bytes 1769480 | tf_op jit(solution)/shard_map/ppermute | solution.py:39
  411.7 38.2 %collective-permute-start.15 = (bf16[1,256,1152]{2,1,0:T(8,128)(2,1)S(1)}, bf16[1,256,1152]{2,1,0:T(8,128)(2,1)}, u32[]{:S(2)}, u32[]{:S(2)}) collective-permute-start(bf16[1,256,1152]{2,1,0:T(8,128)(2,1)S(1)} %get-tuple-element.199), channel_id=1, source_target_pairs={{0,3},{1,0},{2,1},{3,2},{4,7},{5,4},{6,5},{7,6},{8,11},{9,8},{10,9... | collective-permute-start | bytes 1769480 | tf_op jit(solution)/shard_map/ppermute | solution.py:39
  422.2 182.0 %reduce-scatter.5.cloned.1.call-start = ((), (), s32[]{:S(2)}) async-start(), calls=%async_computation.5 | async-start | bytes 2985984 | tf_op jit(solution)/shard_map/reduce_scatter | solution.py:250
  428.1 25.3 %copy-start.45 = (f32[1152]{0:T(1024)S(1)}, f32[1152]{0:T(1024)}, u32[]{:S(2)}) copy-start(f32[1152]{0:T(1024)} %get-tuple-element.149) | copy-start | bytes 13828
  454.3 39.0 %collective-permute-start.16 = (bf16[1,256,1152]{2,1,0:T(8,128)(2,1)S(1)}, bf16[1,256,1152]{2,1,0:T(8,128)(2,1)S(1)}, u32[]{:S(2)}, u32[]{:S(2)}) collective-permute-start(bf16[1,256,1152]{2,1,0:T(8,128)(2,1)S(1)} %get-tuple-element.174), channel_id=1, source_target_pairs={{0,1},{1,2},{2,3},{3,0},{4,5},{5,6},{6,7},{7,4},{8,9},{9,10},{10,1... | collective-permute-start | bytes 1769480 | tf_op jit(solution)/shard_map/ppermute | solution.py:39
  467.4 36.7 %collective-permute-start.17 = (bf16[1,256,1152]{2,1,0:T(8,128)(2,1)S(1)}, bf16[1,256,1152]{2,1,0:T(8,128)(2,1)S(1)}, u32[]{:S(2)}, u32[]{:S(2)}) collective-permute-start(bf16[1,256,1152]{2,1,0:T(8,128)(2,1)S(1)} %get-tuple-element.174), channel_id=1, source_target_pairs={{0,2},{1,3},{2,0},{3,1},{4,6},{5,7},{6,4},{7,5},{8,10},{9,11},{10,... | collective-permute-start | bytes 1769480 | tf_op jit(solution)/shard_map/ppermute | solution.py:39
  467.4 38.1 %collective-permute-start.18 = (bf16[1,256,1152]{2,1,0:T(8,128)(2,1)S(1)}, bf16[1,256,1152]{2,1,0:T(8,128)(2,1)S(1)}, u32[]{:S(2)}, u32[]{:S(2)}) collective-permute-start(bf16[1,256,1152]{2,1,0:T(8,128)(2,1)S(1)} %get-tuple-element.174), channel_id=1, source_target_pairs={{0,3},{1,0},{2,1},{3,2},{4,7},{5,4},{6,5},{7,6},{8,11},{9,8},{10,9... | collective-permute-start | bytes 1769480 | tf_op jit(solution)/shard_map/ppermute | solution.py:39
  509.0 27.3 %collective-permute-start.19 = (bf16[1,1024,2,288]{1,3,2,0:T(8,128)(2,1)S(1)}, bf16[1,1024,2,288]{1,3,2,0:T(8,128)(2,1)S(1)}, u32[]{:S(2)}, u32[]{:S(2)}) collective-permute-start(bf16[1,1024,2,288]{1,3,2,0:T(8,128)(2,1)S(1)} %fusion.37), channel_id=1, source_target_pairs={{0,4},{4,0},{1,5},{5,1},{2,6},{6,2},{3,7},{7,3},{8,12},{12,8},{9,1... | collective-permute-start | bytes 3538952 | tf_op jit(solution)/shard_map/ppermute | solution.py:39
  510.6 27.2 %copy-start.3 = (bf16[1,1024,1152]{2,1,0:T(8,128)(2,1)S(1)}, bf16[1,1024,1152]{2,1,0:T(8,128)(2,1)}, u32[]{:S(2)}) copy-start(bf16[1,1024,1152]{2,1,0:T(8,128)(2,1)} %param.10) | copy-start | bytes 7077892
  510.6 27.2 %copy-start.42 = (f32[1152]{0:T(1024)S(1)}, f32[1152]{0:T(1024)}, u32[]{:S(2)}) copy-start(f32[1152]{0:T(1024)} %copy-done.41) | copy-start | bytes 13828
  510.6 27.1 %copy-start.53 = (f32[1024]{0:T(1024)S(1)}, f32[1024]{0:T(1024)}, u32[]{:S(2)}) copy-start(f32[1024]{0:T(1024)} %copy-done.52) | copy-start | bytes 12292
  510.6 27.1 %copy-start.59 = (f32[1152]{0:T(1024)S(1)}, f32[1152]{0:T(1024)}, u32[]{:S(2)}) copy-start(f32[1152]{0:T(1024)} %copy-done.58) | copy-start | bytes 13828
  510.6 27.1 %copy-start.63 = (f32[1024]{0:T(1024)S(1)}, f32[1024]{0:T(1024)}, u32[]{:S(2)}) copy-start(f32[1024]{0:T(1024)} %copy-done.62) | copy-start | bytes 12292
  549.7 31.1 %collective-permute-start.20 = (bf16[1,256,1152]{2,1,0:T(8,128)(2,1)S(1)}, bf16[1,256,1152]{2,1,0:T(8,128)(2,1)S(1)}, u32[]{:S(2)}, u32[]{:S(2)}) collective-permute-start(bf16[1,256,1152]{2,1,0:T(8,128)(2,1)S(1)} %get-tuple-element.189), channel_id=1, source_target_pairs={{0,1},{1,2},{2,3},{3,0},{4,5},{5,6},{6,7},{7,4},{8,9},{9,10},{10,1... | collective-permute-start | bytes 1769480 | tf_op jit(solution)/shard_map/ppermute | solution.py:39
  563.6 40.3 %collective-permute-start.21 = (bf16[1,256,1152]{2,1,0:T(8,128)(2,1)S(1)}, bf16[1,256,1152]{2,1,0:T(8,128)(2,1)S(1)}, u32[]{:S(2)}, u32[]{:S(2)}) collective-permute-start(bf16[1,256,1152]{2,1,0:T(8,128)(2,1)S(1)} %get-tuple-element.191), channel_id=1, source_target_pairs={{0,2},{1,3},{2,0},{3,1},{4,6},{5,7},{6,4},{7,5},{8,10},{9,11},{10,... | collective-permute-start | bytes 1769480 | tf_op jit(solution)/shard_map/ppermute | solution.py:39
  567.0 36.9 %collective-permute-start.22 = (bf16[1,256,1152]{2,1,0:T(8,128)(2,1)S(1)}, bf16[1,256,1152]{2,1,0:T(8,128)(2,1)S(1)}, u32[]{:S(2)}, u32[]{:S(2)}) collective-permute-start(bf16[1,256,1152]{2,1,0:T(8,128)(2,1)S(1)} %get-tuple-element.190), channel_id=1, source_target_pairs={{0,3},{1,0},{2,1},{3,2},{4,7},{5,4},{6,5},{7,6},{8,11},{9,8},{10,9... | collective-permute-start | bytes 1769480 | tf_op jit(solution)/shard_map/ppermute | solution.py:39
  568.9 35.3 %copy-start.56 = (f32[256]{0:T(256)S(1)}, f32[256]{0:T(256)}, u32[]{:S(2)}) copy-start(f32[256]{0:T(256)} %broadcast_multiply_fusion.1) | copy-start | bytes 3076
  608.0 83.6 %copy-start.51 = (bf16[4,1,288]{2,1,0:T(2,128)(2,1)S(1)}, bf16[4,1,288]{2,1,0:T(2,128)(2,1)}, u32[]{:S(2)}) copy-start(bf16[4,1,288]{2,1,0:T(2,128)(2,1)} %copy-done.50) | copy-start | bytes 6916
  608.0 100.2 %copy-start.60 = (bf16[1,288]{1,0:T(2,128)(2,1)S(1)}, bf16[1,288]{1,0:T(2,128)(2,1)}, u32[]{:S(2)}) copy-start(bf16[1,288]{1,0:T(2,128)(2,1)} %param.11) | copy-start | bytes 1732
  608.0 100.2 %copy-start.61 = (f32[1,288]{1,0:T(1,128)S(1)}, f32[1,288]{1,0:T(1,128)}, u32[]{:S(2)}) copy-start(f32[1,288]{1,0:T(1,128)} %get-tuple-element.185) | copy-start | bytes 3460
  609.0 101.6 %collective-permute-start.23 = (bf16[1,256,1152]{2,1,0:T(8,128)(2,1)}, bf16[1,256,1152]{2,1,0:T(8,128)(2,1)}, u32[]{:S(2)}, u32[]{:S(2)}) collective-permute-start(bf16[1,256,1152]{2,1,0:T(8,128)(2,1)} %get-tuple-element.170), channel_id=1, source_target_pairs={{0,1},{1,2},{2,3},{3,0},{4,5},{5,6},{6,7},{7,4},{8,9},{9,10},{10,1... | collective-permute-start | bytes 1769480 | tf_op jit(solution)/shard_map/ppermute | solution.py:39
  622.1 89.7 %collective-permute-start.24 = (bf16[1,256,1152]{2,1,0:T(8,128)(2,1)}, bf16[1,256,1152]{2,1,0:T(8,128)(2,1)}, u32[]{:S(2)}, u32[]{:S(2)}) collective-permute-start(bf16[1,256,1152]{2,1,0:T(8,128)(2,1)} %get-tuple-element.170), channel_id=1, source_target_pairs={{0,2},{1,3},{2,0},{3,1},{4,6},{5,7},{6,4},{7,5},{8,10},{9,11},{10,... | collective-permute-start | bytes 1769480 | tf_op jit(solution)/shard_map/ppermute | solution.py:39
  622.1 90.8 %collective-permute-start.25 = (bf16[1,256,1152]{2,1,0:T(8,128)(2,1)}, bf16[1,256,1152]{2,1,0:T(8,128)(2,1)}, u32[]{:S(2)}, u32[]{:S(2)}) collective-permute-start(bf16[1,256,1152]{2,1,0:T(8,128)(2,1)} %get-tuple-element.170), channel_id=1, source_target_pairs={{0,3},{1,0},{2,1},{3,2},{4,7},{5,4},{6,5},{7,6},{8,11},{9,8},{10,9... | collective-permute-start | bytes 1769480 | tf_op jit(solution)/shard_map/ppermute | solution.py:39
  (53 other events, 256.6 us)
Sparse Core Ops, SparseCore 0:
  9.9 33.4 all-gather.10
  57.1 53.3 all-gather.12
  422.3 61.1 reduce-scatter.2
  543.2 57.7 reduce-scatter.4
